TPU v7x, 512 devices: a whole 4x4x16 slice. The times are simulated.
512 devices in a mesh: pts: 512 (over y, x, z, core).
Axes of the slice: x: 4, y: 4, z: 16, core: 2. Of those that a mesh axis runs over, the one named last changes fastest.
Arguments:
- points: bfloat16 [64, 1048576], P(None, 'pts'), may hold values from -6 to 6
- inv_scale: float32 [64], replicated, may hold values from 0.05 to 0.25
- vectors: bfloat16 [32, 1048576], P(None, 'pts'), may hold values from -0.59765625 to 0.59765625
Outputs:
- product: float32 [32, 1048576], P(None, 'pts')
All inputs are finite; a program needn't handle non-finite values.
Results may differ from a plain program's by a relative error of at most 0.0003.
Values sent between devices are 32-bit elements; how exact they have to be, the bound alone decides.
No kernel may reach another device: no remote copies, remote signals or barrier semaphores. Data moves between devices by JAX's collectives and lax.ppermute only.
A program may use at most 64 MiB of HBM per device.

v0:
```python
import jax
import jax.numpy as jnp
from jax import lax
from jax.sharding import PartitionSpec as P

ROUNDS = 2


def shifted(value, axis, steps):
    count = lax.axis_size(axis)
    pairs = [(source, (source + steps) % count) for source in range(count)]
    return lax.ppermute(value, axis, pairs)


def tile_products(rows, cols, vec_rows, vec_cols, need_back):
    row_count = rows.shape[1]
    step_rows = min(512, row_count)
    count = row_count // step_rows
    sq_cols = jnp.sum(cols * cols, axis=0)
    width = vec_rows.shape[0]

    def one_step(back_total, index):
        start = index * step_rows
        row_part = lax.dynamic_slice_in_dim(rows, start, step_rows, 1)
        sq_rows = jnp.sum(row_part * row_part, axis=0)
        cross = lax.dot_general(
            row_part,
            cols,
            (((0,), (0,)), ((), ())),
            precision=lax.Precision.HIGHEST,
            preferred_element_type=jnp.float32,
        )
        kern = jnp.exp(-0.5 * (sq_rows[:, None] + sq_cols[None, :] - 2.0 * cross))
        forward = lax.dot_general(
            vec_cols,
            kern,
            (((1,), (1,)), ((), ())),
            precision=lax.Precision.HIGHEST,
            preferred_element_type=jnp.float32,
        )
        if need_back:
            vec_part = lax.dynamic_slice_in_dim(vec_rows, start, step_rows, 1)
            back_total = back_total + lax.dot_general(
                vec_part,
                kern,
                (((1,), (0,)), ((), ())),
                precision=lax.Precision.HIGHEST,
                preferred_element_type=jnp.float32,
            )
        return (back_total, forward)

    start_back = jnp.zeros((width, cols.shape[1]), jnp.float32)
    back_total, forwards = lax.scan(one_step, start_back, jnp.arange(count, dtype=jnp.int32))
    forward_all = jnp.transpose(forwards, (1, 0, 2)).reshape(width, row_count)
    return (forward_all, back_total)


def per_device(points, inv_scale, vectors):
    scaled = points.astype(jnp.float32) * inv_scale[:, None]
    vec_full = vectors.astype(jnp.float32)
    total, unused = tile_products(scaled, scaled, vec_full, vec_full, False)
    for step in range(1, ROUNDS + 1):
        got_points, got_vectors = shifted((scaled, vec_full), "pts", -step)
        forward, back = tile_products(scaled, got_points, vec_full, got_vectors, True)
        total = total + forward
        returned = shifted(back, "pts", step)
        total = total + returned
    return total


def solution(mesh):
    return jax.shard_map(
        per_device,
        mesh=mesh,
        in_specs=(P(None, "pts"), P(), P(None, "pts")),
        out_specs=P(None, "pts"),
        check_vma=False,
    )
```

profile of v0, /device:TPU:1, one launch (start us, length us, event | category | flops | bytes accessed | tf_op | source)
XLA Modules:
  0.0 228.6 jit_solution(5528426535049978793)
XLA Ops:
  0.0 1.9 multiply_reduce_fusion.5
  1.9 8.8 %collective-permute-start = (f32[64,2048]{1,0:T(8,128)}, f32[64,2048]{1,0:T(8,128)S(1)}, u32[]{:S(2)}, u32[]{:S(2)}) collective-permute-start(f32[64,2048]{1,0:T(8,128)} %get-tuple-element.469), channel_id=1, source_target_pairs={{0,511},{1,0},{2,1},{3,2},{4,3},{5,4},{6,5},{7,6},{8,7},{9,8},{10,... | collective-permute-start | bytes 1572872 | tf_op jit(solution)/shard_map/ppermute | solution.py:12
  10.7 1.6 convert_element_type.7
  12.3 10.1 %collective-permute-start.1 = (f32[32,2048]{1,0:T(8,128)}, f32[32,2048]{1,0:T(8,128)S(1)}, u32[]{:S(2)}, u32[]{:S(2)}) collective-permute-start(f32[32,2048]{1,0:T(8,128)} %convert_element_type.7), channel_id=1, source_target_pairs={{0,511},{1,0},{2,1},{3,2},{4,3},{5,4},{6,5},{7,6},{8,7},{9,8},{10,... | collective-permute-start | bytes 786440 | tf_op jit(solution)/shard_map/ppermute | solution.py:12
  22.4 2.6 %collective-permute-start.3 = (f32[64,2048]{1,0:T(8,128)}, f32[64,2048]{1,0:T(8,128)S(1)}, u32[]{:S(2)}, u32[]{:S(2)}) collective-permute-start(f32[64,2048]{1,0:T(8,128)} %get-tuple-element.469), channel_id=1, source_target_pairs={{0,510},{1,511},{2,0},{3,1},{4,2},{5,3},{6,4},{7,5},{8,6},{9,7},{1... | collective-permute-start | bytes 1572872 | tf_op jit(solution)/shard_map/ppermute | solution.py:12
  25.1 2.6 %collective-permute-start.4 = (f32[32,2048]{1,0:T(8,128)}, f32[32,2048]{1,0:T(8,128)S(1)}, u32[]{:S(2)}, u32[]{:S(2)}) collective-permute-start(f32[32,2048]{1,0:T(8,128)} %convert_element_type.7), channel_id=1, source_target_pairs={{0,510},{1,511},{2,0},{3,1},{4,2},{5,3},{6,4},{7,5},{8,6},{9,7},{1... | collective-permute-start | bytes 786440 | tf_op jit(solution)/shard_map/ppermute | solution.py:12
  27.8 71.1 %while.37 = (s32[]{:T(128)}, f32[32,2048]{1,0:T(8,128)S(1)}, f32[4,32,512]{2,1,0:T(8,128)S(1)}, s32[4]{0:T(128)S(1)}, f32[32,2048]{1,0:T(8,128)}, /*index=5*/f32...) while((s32[]{:T(128)}, f32[32,2048]{1,0:T(8,128)S(1)}, ...), condition=%wide.region_7.8_spmd.clone, body=%wide.region_5.7_spmd.clone.sunk | while | flops 1615003136 | bytes 31076588 | solution.py:53
  30.2 6.7 %multiply_exponential_fusion.4 = f32[512,2048]{1,0:T(8,128)} fusion(f32[64,2048]{1,0:T(8,128)S(1)} %get-tuple-element.497, f32[2048]{0:T(1024)S(1)} %get-tuple-element.496, f32[512]{0:T(512)S(1)} %multiply_reduce_fusion.10, f32[64,2048]{1,0:T(8,128)} %get-tuple-element.495, s32[]{:T(128)S(6)} %select_n.17), kind=kOutput, calls=%fused_computation.18.clone.1 | convolution fusion | flops 809500672 | bytes 4859908 | tf_op jit(solution)/shard_map/while/body/eval_jaxpr/dot_general | solution.py:26
  36.8 4.9 %convolution_add_fusion.4 = f32[32,2048]{1,0:T(8,128)S(1)} fusion(f32[512,2048]{1,0:T(8,128)} %multiply_exponential_fusion.4, f32[32,2048]{1,0:T(8,128)S(1)} %get-tuple-element.478, pred[]{:T(512)S(6)} %compare.6, f32[32,2048]{1,0:T(8,128)} %get-tuple-element.494, s32[]{:T(128)S(6)} %select_n.17), kind=kOutput, calls=%fused_computation.19.clone.1 | convolution fusion | flops 402784256 | bytes 4784133 | tf_op jit(solution)/shard_map/while/body/eval_jaxpr/dot_general | solution.py:43
  41.7 3.9 %fusion.73 = f32[4,32,512]{2,1,0:T(8,128)S(1)} fusion(f32[4,32,512]{2,1,0:T(8,128)S(1)} %get-tuple-element.479, s32[]{:T(128)} %get-tuple-element.477, f32[512,2048]{1,0:T(8,128)S(1)} %copy-done, f32[32,2048]{1,0:T(8,128)S(1)} %get-tuple-element.498), kind=kOutput, calls=%fused_computation.21.clone.1 | convolution fusion | flops 402653184 | bytes 4521988 | tf_op jit(solution)/shard_map/while/body/eval_jaxpr/dot_general | solution.py:34
  47.0 0.9 multiply_reduce_fusion.10
  47.9 6.6 %multiply_exponential_fusion.4 = f32[512,2048]{1,0:T(8,128)} fusion(f32[64,2048]{1,0:T(8,128)S(1)} %get-tuple-element.497, f32[2048]{0:T(1024)S(1)} %get-tuple-element.496, f32[512]{0:T(512)S(1)} %multiply_reduce_fusion.10, f32[64,2048]{1,0:T(8,128)} %get-tuple-element.495, s32[]{:T(128)S(6)} %select_n.17), kind=kOutput, calls=%fused_computation.18.clone.1 | convolution fusion | flops 809500672 | bytes 4859908 | tf_op jit(solution)/shard_map/while/body/eval_jaxpr/dot_general | solution.py:26
  54.6 4.9 %convolution_add_fusion.4 = f32[32,2048]{1,0:T(8,128)S(1)} fusion(f32[512,2048]{1,0:T(8,128)} %multiply_exponential_fusion.4, f32[32,2048]{1,0:T(8,128)S(1)} %get-tuple-element.478, pred[]{:T(512)S(6)} %compare.6, f32[32,2048]{1,0:T(8,128)} %get-tuple-element.494, s32[]{:T(128)S(6)} %select_n.17), kind=kOutput, calls=%fused_computation.19.clone.1 | convolution fusion | flops 402784256 | bytes 4784133 | tf_op jit(solution)/shard_map/while/body/eval_jaxpr/dot_general | solution.py:43
  59.5 3.9 %fusion.73 = f32[4,32,512]{2,1,0:T(8,128)S(1)} fusion(f32[4,32,512]{2,1,0:T(8,128)S(1)} %get-tuple-element.479, s32[]{:T(128)} %get-tuple-element.477, f32[512,2048]{1,0:T(8,128)S(1)} %copy-done, f32[32,2048]{1,0:T(8,128)S(1)} %get-tuple-element.498), kind=kOutput, calls=%fused_computation.21.clone.1 | convolution fusion | flops 402653184 | bytes 4521988 | tf_op jit(solution)/shard_map/while/body/eval_jaxpr/dot_general | solution.py:34
  64.8 0.9 multiply_reduce_fusion.10
  65.7 6.6 %multiply_exponential_fusion.4 = f32[512,2048]{1,0:T(8,128)} fusion(f32[64,2048]{1,0:T(8,128)S(1)} %get-tuple-element.497, f32[2048]{0:T(1024)S(1)} %get-tuple-element.496, f32[512]{0:T(512)S(1)} %multiply_reduce_fusion.10, f32[64,2048]{1,0:T(8,128)} %get-tuple-element.495, s32[]{:T(128)S(6)} %select_n.17), kind=kOutput, calls=%fused_computation.18.clone.1 | convolution fusion | flops 809500672 | bytes 4859908 | tf_op jit(solution)/shard_map/while/body/eval_jaxpr/dot_general | solution.py:26
  72.3 4.9 %convolution_add_fusion.4 = f32[32,2048]{1,0:T(8,128)S(1)} fusion(f32[512,2048]{1,0:T(8,128)} %multiply_exponential_fusion.4, f32[32,2048]{1,0:T(8,128)S(1)} %get-tuple-element.478, pred[]{:T(512)S(6)} %compare.6, f32[32,2048]{1,0:T(8,128)} %get-tuple-element.494, s32[]{:T(128)S(6)} %select_n.17), kind=kOutput, calls=%fused_computation.19.clone.1 | convolution fusion | flops 402784256 | bytes 4784133 | tf_op jit(solution)/shard_map/while/body/eval_jaxpr/dot_general | solution.py:43
  77.2 3.9 %fusion.73 = f32[4,32,512]{2,1,0:T(8,128)S(1)} fusion(f32[4,32,512]{2,1,0:T(8,128)S(1)} %get-tuple-element.479, s32[]{:T(128)} %get-tuple-element.477, f32[512,2048]{1,0:T(8,128)S(1)} %copy-done, f32[32,2048]{1,0:T(8,128)S(1)} %get-tuple-element.498), kind=kOutput, calls=%fused_computation.21.clone.1 | convolution fusion | flops 402653184 | bytes 4521988 | tf_op jit(solution)/shard_map/while/body/eval_jaxpr/dot_general | solution.py:34
  82.5 0.9 multiply_reduce_fusion.10
  83.5 6.6 %multiply_exponential_fusion.4 = f32[512,2048]{1,0:T(8,128)} fusion(f32[64,2048]{1,0:T(8,128)S(1)} %get-tuple-element.497, f32[2048]{0:T(1024)S(1)} %get-tuple-element.496, f32[512]{0:T(512)S(1)} %multiply_reduce_fusion.10, f32[64,2048]{1,0:T(8,128)} %get-tuple-element.495, s32[]{:T(128)S(6)} %select_n.17), kind=kOutput, calls=%fused_computation.18.clone.1 | convolution fusion | flops 809500672 | bytes 4859908 | tf_op jit(solution)/shard_map/while/body/eval_jaxpr/dot_general | solution.py:26
  90.1 4.9 %convolution_add_fusion.4 = f32[32,2048]{1,0:T(8,128)S(1)} fusion(f32[512,2048]{1,0:T(8,128)} %multiply_exponential_fusion.4, f32[32,2048]{1,0:T(8,128)S(1)} %get-tuple-element.478, pred[]{:T(512)S(6)} %compare.6, f32[32,2048]{1,0:T(8,128)} %get-tuple-element.494, s32[]{:T(128)S(6)} %select_n.17), kind=kOutput, calls=%fused_computation.19.clone.1 | convolution fusion | flops 402784256 | bytes 4784133 | tf_op jit(solution)/shard_map/while/body/eval_jaxpr/dot_general | solution.py:43
  95.0 3.9 %fusion.73 = f32[4,32,512]{2,1,0:T(8,128)S(1)} fusion(f32[4,32,512]{2,1,0:T(8,128)S(1)} %get-tuple-element.479, s32[]{:T(128)} %get-tuple-element.477, f32[512,2048]{1,0:T(8,128)S(1)} %copy-done, f32[32,2048]{1,0:T(8,128)S(1)} %get-tuple-element.498), kind=kOutput, calls=%fused_computation.21.clone.1 | convolution fusion | flops 402653184 | bytes 4521988 | tf_op jit(solution)/shard_map/while/body/eval_jaxpr/dot_general | solution.py:34
  98.9 3.9 %collective-permute-start.2 = (f32[32,2048]{1,0:T(8,128)S(1)}, f32[32,2048]{1,0:T(8,128)S(1)}, u32[]{:S(2)}, u32[]{:S(2)}) collective-permute-start(f32[32,2048]{1,0:T(8,128)S(1)} %get-tuple-element.135), channel_id=1, source_target_pairs={{0,1},{1,2},{2,3},{3,4},{4,5},{5,6},{6,7},{7,8},{8,9},{9,10},{10,1... | collective-permute-start | bytes 786440 | tf_op jit(solution)/shard_map/ppermute | solution.py:12
  103.0 71.1 %while.38 = (s32[]{:T(128)}, f32[32,2048]{1,0:T(8,128)S(1)}, f32[4,32,512]{2,1,0:T(8,128)S(1)}, s32[4]{0:T(128)S(1)}, f32[32,2048]{1,0:T(8,128)}, /*index=5*/f32...) while((s32[]{:T(128)}, f32[32,2048]{1,0:T(8,128)S(1)}, ...), condition=%wide.region_11.12_spmd.clone, body=%wide.region_9.11_spmd.clone.sunk | while | flops 1615003136 | bytes 31076588 | solution.py:53
  105.3 6.6 %multiply_exponential_fusion.5 = f32[512,2048]{1,0:T(8,128)} fusion(f32[64,2048]{1,0:T(8,128)S(1)} %get-tuple-element.428, f32[2048]{0:T(1024)S(1)} %get-tuple-element.427, f32[512]{0:T(512)S(1)} %multiply_reduce_fusion.11, f32[64,2048]{1,0:T(8,128)} %get-tuple-element.426, s32[]{:T(128)S(6)} %select_n.18), kind=kOutput, calls=%fused_computation.27.clone.1 | convolution fusion | flops 809500672 | bytes 4859908 | tf_op jit(solution)/shard_map/while/body/eval_jaxpr/dot_general | solution.py:26
  112.0 4.9 %convolution_add_fusion.5 = f32[32,2048]{1,0:T(8,128)S(1)} fusion(f32[512,2048]{1,0:T(8,128)} %multiply_exponential_fusion.5, f32[32,2048]{1,0:T(8,128)S(1)} %get-tuple-element.409, pred[]{:T(512)S(6)} %compare.7, f32[32,2048]{1,0:T(8,128)} %get-tuple-element.425, s32[]{:T(128)S(6)} %select_n.18), kind=kOutput, calls=%fused_computation.28.clone.1 | convolution fusion | flops 402784256 | bytes 4784133 | tf_op jit(solution)/shard_map/while/body/eval_jaxpr/dot_general | solution.py:43
  116.8 3.9 %fusion.80 = f32[4,32,512]{2,1,0:T(8,128)S(1)} fusion(f32[4,32,512]{2,1,0:T(8,128)S(1)} %get-tuple-element.410, s32[]{:T(128)} %get-tuple-element.408, f32[512,2048]{1,0:T(8,128)S(1)} %copy-done.1, f32[32,2048]{1,0:T(8,128)S(1)} %get-tuple-element.429), kind=kOutput, calls=%fused_computation.30.clone.1 | convolution fusion | flops 402653184 | bytes 4521988 | tf_op jit(solution)/shard_map/while/body/eval_jaxpr/dot_general | solution.py:34
  123.1 6.6 %multiply_exponential_fusion.5 = f32[512,2048]{1,0:T(8,128)} fusion(f32[64,2048]{1,0:T(8,128)S(1)} %get-tuple-element.428, f32[2048]{0:T(1024)S(1)} %get-tuple-element.427, f32[512]{0:T(512)S(1)} %multiply_reduce_fusion.11, f32[64,2048]{1,0:T(8,128)} %get-tuple-element.426, s32[]{:T(128)S(6)} %select_n.18), kind=kOutput, calls=%fused_computation.27.clone.1 | convolution fusion | flops 809500672 | bytes 4859908 | tf_op jit(solution)/shard_map/while/body/eval_jaxpr/dot_general | solution.py:26
  129.7 4.9 %convolution_add_fusion.5 = f32[32,2048]{1,0:T(8,128)S(1)} fusion(f32[512,2048]{1,0:T(8,128)} %multiply_exponential_fusion.5, f32[32,2048]{1,0:T(8,128)S(1)} %get-tuple-element.409, pred[]{:T(512)S(6)} %compare.7, f32[32,2048]{1,0:T(8,128)} %get-tuple-element.425, s32[]{:T(128)S(6)} %select_n.18), kind=kOutput, calls=%fused_computation.28.clone.1 | convolution fusion | flops 402784256 | bytes 4784133 | tf_op jit(solution)/shard_map/while/body/eval_jaxpr/dot_general | solution.py:43
  134.6 3.9 %fusion.80 = f32[4,32,512]{2,1,0:T(8,128)S(1)} fusion(f32[4,32,512]{2,1,0:T(8,128)S(1)} %get-tuple-element.410, s32[]{:T(128)} %get-tuple-element.408, f32[512,2048]{1,0:T(8,128)S(1)} %copy-done.1, f32[32,2048]{1,0:T(8,128)S(1)} %get-tuple-element.429), kind=kOutput, calls=%fused_computation.30.clone.1 | convolution fusion | flops 402653184 | bytes 4521988 | tf_op jit(solution)/shard_map/while/body/eval_jaxpr/dot_general | solution.py:34
  140.8 6.6 %multiply_exponential_fusion.5 = f32[512,2048]{1,0:T(8,128)} fusion(f32[64,2048]{1,0:T(8,128)S(1)} %get-tuple-element.428, f32[2048]{0:T(1024)S(1)} %get-tuple-element.427, f32[512]{0:T(512)S(1)} %multiply_reduce_fusion.11, f32[64,2048]{1,0:T(8,128)} %get-tuple-element.426, s32[]{:T(128)S(6)} %select_n.18), kind=kOutput, calls=%fused_computation.27.clone.1 | convolution fusion | flops 809500672 | bytes 4859908 | tf_op jit(solution)/shard_map/while/body/eval_jaxpr/dot_general | solution.py:26
  147.5 4.9 %convolution_add_fusion.5 = f32[32,2048]{1,0:T(8,128)S(1)} fusion(f32[512,2048]{1,0:T(8,128)} %multiply_exponential_fusion.5, f32[32,2048]{1,0:T(8,128)S(1)} %get-tuple-element.409, pred[]{:T(512)S(6)} %compare.7, f32[32,2048]{1,0:T(8,128)} %get-tuple-element.425, s32[]{:T(128)S(6)} %select_n.18), kind=kOutput, calls=%fused_computation.28.clone.1 | convolution fusion | flops 402784256 | bytes 4784133 | tf_op jit(solution)/shard_map/while/body/eval_jaxpr/dot_general | solution.py:43
  152.4 3.9 %fusion.80 = f32[4,32,512]{2,1,0:T(8,128)S(1)} fusion(f32[4,32,512]{2,1,0:T(8,128)S(1)} %get-tuple-element.410, s32[]{:T(128)} %get-tuple-element.408, f32[512,2048]{1,0:T(8,128)S(1)} %copy-done.1, f32[32,2048]{1,0:T(8,128)S(1)} %get-tuple-element.429), kind=kOutput, calls=%fused_computation.30.clone.1 | convolution fusion | flops 402653184 | bytes 4521988 | tf_op jit(solution)/shard_map/while/body/eval_jaxpr/dot_general | solution.py:34
  158.6 6.6 %multiply_exponential_fusion.5 = f32[512,2048]{1,0:T(8,128)} fusion(f32[64,2048]{1,0:T(8,128)S(1)} %get-tuple-element.428, f32[2048]{0:T(1024)S(1)} %get-tuple-element.427, f32[512]{0:T(512)S(1)} %multiply_reduce_fusion.11, f32[64,2048]{1,0:T(8,128)} %get-tuple-element.426, s32[]{:T(128)S(6)} %select_n.18), kind=kOutput, calls=%fused_computation.27.clone.1 | convolution fusion | flops 809500672 | bytes 4859908 | tf_op jit(solution)/shard_map/while/body/eval_jaxpr/dot_general | solution.py:26
  165.3 4.9 %convolution_add_fusion.5 = f32[32,2048]{1,0:T(8,128)S(1)} fusion(f32[512,2048]{1,0:T(8,128)} %multiply_exponential_fusion.5, f32[32,2048]{1,0:T(8,128)S(1)} %get-tuple-element.409, pred[]{:T(512)S(6)} %compare.7, f32[32,2048]{1,0:T(8,128)} %get-tuple-element.425, s32[]{:T(128)S(6)} %select_n.18), kind=kOutput, calls=%fused_computation.28.clone.1 | convolution fusion | flops 402784256 | bytes 4784133 | tf_op jit(solution)/shard_map/while/body/eval_jaxpr/dot_general | solution.py:43
  170.1 3.9 %fusion.80 = f32[4,32,512]{2,1,0:T(8,128)S(1)} fusion(f32[4,32,512]{2,1,0:T(8,128)S(1)} %get-tuple-element.410, s32[]{:T(128)} %get-tuple-element.408, f32[512,2048]{1,0:T(8,128)S(1)} %copy-done.1, f32[32,2048]{1,0:T(8,128)S(1)} %get-tuple-element.429), kind=kOutput, calls=%fused_computation.30.clone.1 | convolution fusion | flops 402653184 | bytes 4521988 | tf_op jit(solution)/shard_map/while/body/eval_jaxpr/dot_general | solution.py:34
  174.1 2.9 %collective-permute-start.5 = (f32[32,2048]{1,0:T(8,128)S(1)}, f32[32,2048]{1,0:T(8,128)S(1)}, u32[]{:S(2)}, u32[]{:S(2)}) collective-permute-start(f32[32,2048]{1,0:T(8,128)S(1)} %get-tuple-element.137), channel_id=1, source_target_pairs={{0,2},{1,3},{2,4},{3,5},{4,6},{5,7},{6,8},{7,9},{8,10},{9,11},{10,... | collective-permute-start | bytes 786440 | tf_op jit(solution)/shard_map/ppermute | solution.py:12
  177.0 50.7 %while.36 = (s32[]{:T(128)}, f32[4,32,512]{2,1,0:T(8,128)S(1)}, s32[4]{0:T(128)S(1)}, f32[64,2048]{1,0:T(8,128)}, f32[2048]{0:T(1024)S(1)}, /*index=5*/f32[32,20...) while((s32[]{:T(128)}, f32[4,32,512]{2,1,0:T(8,128)S(1)}, s32[4]{0:T(128)S(1)}, ...), condition=%wide.region_3.4_spmd, body=%wide.region_1.3_spmd.sunk | while | flops 1212218880 | bytes 9515179 | solution.py:53
  178.4 4.7 %fusion.65 = f32[512,2048]{1,0:T(8,128)S(1)} fusion(f32[64,2048]{1,0:T(8,128)} %get-tuple-element.457, s32[]{:T(128)S(6)} %select_n.16), kind=kOutput, calls=%fused_computation.13.clone.1 | convolution fusion | flops 805306368 | bytes 4849668 | tf_op jit(solution)/shard_map/while/body/eval_jaxpr/dot_general | solution.py:26
  184.0 5.7 %fusion.66 = f32[4,32,512]{2,1,0:T(8,128)S(1)} fusion(f32[4,32,512]{2,1,0:T(8,128)S(1)} %get-tuple-element.445, s32[]{:T(128)} %get-tuple-element.444, f32[32,2048]{1,0:T(8,128)} %get-tuple-element.459, f32[512,2048]{1,0:T(8,128)S(1)} %fusion.65, f32[2048]{0:T(1024)S(1)} %get-tuple-element.458, f32[512]{0:T(512)S(1)} %multiply_reduce_fusion.9), kind=kOutput, calls=%fused_computation.11.clone.1 | convolution fusion | flops 406847488 | bytes 4532228 | tf_op jit(solution)/shard_map/while/body/eval_jaxpr/dot_general | solution.py:34
  191.1 4.7 %fusion.65 = f32[512,2048]{1,0:T(8,128)S(1)} fusion(f32[64,2048]{1,0:T(8,128)} %get-tuple-element.457, s32[]{:T(128)S(6)} %select_n.16), kind=kOutput, calls=%fused_computation.13.clone.1 | convolution fusion | flops 805306368 | bytes 4849668 | tf_op jit(solution)/shard_map/while/body/eval_jaxpr/dot_general | solution.py:26
  196.7 5.7 %fusion.66 = f32[4,32,512]{2,1,0:T(8,128)S(1)} fusion(f32[4,32,512]{2,1,0:T(8,128)S(1)} %get-tuple-element.445, s32[]{:T(128)} %get-tuple-element.444, f32[32,2048]{1,0:T(8,128)} %get-tuple-element.459, f32[512,2048]{1,0:T(8,128)S(1)} %fusion.65, f32[2048]{0:T(1024)S(1)} %get-tuple-element.458, f32[512]{0:T(512)S(1)} %multiply_reduce_fusion.9), kind=kOutput, calls=%fused_computation.11.clone.1 | convolution fusion | flops 406847488 | bytes 4532228 | tf_op jit(solution)/shard_map/while/body/eval_jaxpr/dot_general | solution.py:34
  203.7 4.7 %fusion.65 = f32[512,2048]{1,0:T(8,128)S(1)} fusion(f32[64,2048]{1,0:T(8,128)} %get-tuple-element.457, s32[]{:T(128)S(6)} %select_n.16), kind=kOutput, calls=%fused_computation.13.clone.1 | convolution fusion | flops 805306368 | bytes 4849668 | tf_op jit(solution)/shard_map/while/body/eval_jaxpr/dot_general | solution.py:26
  208.4 0.9 multiply_reduce_fusion.9
  209.3 5.7 %fusion.66 = f32[4,32,512]{2,1,0:T(8,128)S(1)} fusion(f32[4,32,512]{2,1,0:T(8,128)S(1)} %get-tuple-element.445, s32[]{:T(128)} %get-tuple-element.444, f32[32,2048]{1,0:T(8,128)} %get-tuple-element.459, f32[512,2048]{1,0:T(8,128)S(1)} %fusion.65, f32[2048]{0:T(1024)S(1)} %get-tuple-element.458, f32[512]{0:T(512)S(1)} %multiply_reduce_fusion.9), kind=kOutput, calls=%fused_computation.11.clone.1 | convolution fusion | flops 406847488 | bytes 4532228 | tf_op jit(solution)/shard_map/while/body/eval_jaxpr/dot_general | solution.py:34
  216.4 4.7 %fusion.65 = f32[512,2048]{1,0:T(8,128)S(1)} fusion(f32[64,2048]{1,0:T(8,128)} %get-tuple-element.457, s32[]{:T(128)S(6)} %select_n.16), kind=kOutput, calls=%fused_computation.13.clone.1 | convolution fusion | flops 805306368 | bytes 4849668 | tf_op jit(solution)/shard_map/while/body/eval_jaxpr/dot_general | solution.py:26
  221.1 0.9 multiply_reduce_fusion.9
  222.0 5.7 %fusion.66 = f32[4,32,512]{2,1,0:T(8,128)S(1)} fusion(f32[4,32,512]{2,1,0:T(8,128)S(1)} %get-tuple-element.445, s32[]{:T(128)} %get-tuple-element.444, f32[32,2048]{1,0:T(8,128)} %get-tuple-element.459, f32[512,2048]{1,0:T(8,128)S(1)} %fusion.65, f32[2048]{0:T(1024)S(1)} %get-tuple-element.458, f32[512]{0:T(512)S(1)} %multiply_reduce_fusion.9), kind=kOutput, calls=%fused_computation.11.clone.1 | convolution fusion | flops 406847488 | bytes 4532228 | tf_op jit(solution)/shard_map/while/body/eval_jaxpr/dot_general | solution.py:34
  (55 shorter events, 15.6 us)
Async XLA Ops:
  1.9 25.8 %collective-permute-start = (f32[64,2048]{1,0:T(8,128)}, f32[64,2048]{1,0:T(8,128)S(1)}, u32[]{:S(2)}, u32[]{:S(2)}) collective-permute-start(f32[64,2048]{1,0:T(8,128)} %get-tuple-element.469), channel_id=1, source_target_pairs={{0,511},{1,0},{2,1},{3,2},{4,3},{5,4},{6,5},{7,6},{8,7},{9,8},{10,... | collective-permute-start | bytes 1572872 | tf_op jit(solution)/shard_map/ppermute | solution.py:12
  12.3 15.5 %collective-permute-start.1 = (f32[32,2048]{1,0:T(8,128)}, f32[32,2048]{1,0:T(8,128)S(1)}, u32[]{:S(2)}, u32[]{:S(2)}) collective-permute-start(f32[32,2048]{1,0:T(8,128)} %convert_element_type.7), channel_id=1, source_target_pairs={{0,511},{1,0},{2,1},{3,2},{4,3},{5,4},{6,5},{7,6},{8,7},{9,8},{10,... | collective-permute-start | bytes 786440 | tf_op jit(solution)/shard_map/ppermute | solution.py:12
  22.4 80.5 %collective-permute-start.3 = (f32[64,2048]{1,0:T(8,128)}, f32[64,2048]{1,0:T(8,128)S(1)}, u32[]{:S(2)}, u32[]{:S(2)}) collective-permute-start(f32[64,2048]{1,0:T(8,128)} %get-tuple-element.469), channel_id=1, source_target_pairs={{0,510},{1,511},{2,0},{3,1},{4,2},{5,3},{6,4},{7,5},{8,6},{9,7},{1... | collective-permute-start | bytes 1572872 | tf_op jit(solution)/shard_map/ppermute | solution.py:12
  25.1 77.9 %collective-permute-start.4 = (f32[32,2048]{1,0:T(8,128)}, f32[32,2048]{1,0:T(8,128)S(1)}, u32[]{:S(2)}, u32[]{:S(2)}) collective-permute-start(f32[32,2048]{1,0:T(8,128)} %convert_element_type.7), channel_id=1, source_target_pairs={{0,510},{1,511},{2,0},{3,1},{4,2},{5,3},{6,4},{7,5},{8,6},{9,7},{1... | collective-permute-start | bytes 786440 | tf_op jit(solution)/shard_map/ppermute | solution.py:12
  36.8 4.9 %copy-start = (f32[512,2048]{1,0:T(8,128)S(1)}, f32[512,2048]{1,0:T(8,128)}, u32[]{:S(2)}) copy-start(f32[512,2048]{1,0:T(8,128)} %multiply_exponential_fusion.4) | copy-start | bytes 12582916 | tf_op jit(solution)/shard_map/while
  54.6 4.9 %copy-start = (f32[512,2048]{1,0:T(8,128)S(1)}, f32[512,2048]{1,0:T(8,128)}, u32[]{:S(2)}) copy-start(f32[512,2048]{1,0:T(8,128)} %multiply_exponential_fusion.4) | copy-start | bytes 12582916 | tf_op jit(solution)/shard_map/while
  72.3 4.9 %copy-start = (f32[512,2048]{1,0:T(8,128)S(1)}, f32[512,2048]{1,0:T(8,128)}, u32[]{:S(2)}) copy-start(f32[512,2048]{1,0:T(8,128)} %multiply_exponential_fusion.4) | copy-start | bytes 12582916 | tf_op jit(solution)/shard_map/while
  90.1 4.9 %copy-start = (f32[512,2048]{1,0:T(8,128)S(1)}, f32[512,2048]{1,0:T(8,128)}, u32[]{:S(2)}) copy-start(f32[512,2048]{1,0:T(8,128)} %multiply_exponential_fusion.4) | copy-start | bytes 12582916 | tf_op jit(solution)/shard_map/while
  98.9 128.9 %collective-permute-start.2 = (f32[32,2048]{1,0:T(8,128)S(1)}, f32[32,2048]{1,0:T(8,128)S(1)}, u32[]{:S(2)}, u32[]{:S(2)}) collective-permute-start(f32[32,2048]{1,0:T(8,128)S(1)} %get-tuple-element.135), channel_id=1, source_target_pairs={{0,1},{1,2},{2,3},{3,4},{4,5},{5,6},{6,7},{7,8},{8,9},{9,10},{10,1... | collective-permute-start | bytes 786440 | tf_op jit(solution)/shard_map/ppermute | solution.py:12
  112.0 4.9 %copy-start.1 = (f32[512,2048]{1,0:T(8,128)S(1)}, f32[512,2048]{1,0:T(8,128)}, u32[]{:S(2)}) copy-start(f32[512,2048]{1,0:T(8,128)} %multiply_exponential_fusion.5) | copy-start | bytes 12582916 | tf_op jit(solution)/shard_map/while
  129.7 4.9 %copy-start.1 = (f32[512,2048]{1,0:T(8,128)S(1)}, f32[512,2048]{1,0:T(8,128)}, u32[]{:S(2)}) copy-start(f32[512,2048]{1,0:T(8,128)} %multiply_exponential_fusion.5) | copy-start | bytes 12582916 | tf_op jit(solution)/shard_map/while
  147.5 4.9 %copy-start.1 = (f32[512,2048]{1,0:T(8,128)S(1)}, f32[512,2048]{1,0:T(8,128)}, u32[]{:S(2)}) copy-start(f32[512,2048]{1,0:T(8,128)} %multiply_exponential_fusion.5) | copy-start | bytes 12582916 | tf_op jit(solution)/shard_map/while
  165.3 4.9 %copy-start.1 = (f32[512,2048]{1,0:T(8,128)S(1)}, f32[512,2048]{1,0:T(8,128)}, u32[]{:S(2)}) copy-start(f32[512,2048]{1,0:T(8,128)} %multiply_exponential_fusion.5) | copy-start | bytes 12582916 | tf_op jit(solution)/shard_map/while
  174.1 53.8 %collective-permute-start.5 = (f32[32,2048]{1,0:T(8,128)S(1)}, f32[32,2048]{1,0:T(8,128)S(1)}, u32[]{:S(2)}, u32[]{:S(2)}) collective-permute-start(f32[32,2048]{1,0:T(8,128)S(1)} %get-tuple-element.137), channel_id=1, source_target_pairs={{0,2},{1,3},{2,4},{3,5},{4,6},{5,7},{6,8},{7,9},{8,10},{9,11},{10,... | collective-permute-start | bytes 786440 | tf_op jit(solution)/shard_map/ppermute | solution.py:12
where the time goes:
time: 230 us; the launch traced here: 229 us
  matrix products  165 us (72%)
  starting transfers between devices  31 us (13%)
  other arithmetic  15.7 us (7%)
  loops' own time  8.85 us (4%)
  local copies, waits for them, and re-layouts  8.13 us (4%)
    dot_general x12, matrix products, one_step(): lax.dot_general(row_part, cols, (((0,), (0,)), ((), ())), precision=lax.P...  71.8 us
    dot_general x12, matrix products, one_step(): lax.dot_general(vec_cols, kern, (((1,), (1,)), ((), ())), precision=lax.P...  54 us
    dot_general x8, matrix products, one_step(): lax.dot_general(vec_part, kern, (((1,), (0,)), ((), ())), precision=lax.P...  38.9 us
    ppermute x6, starting transfers between devices, shifted(): return lax.ppermute(value, axis, pairs)  31 us
    reduce_sum x12, other arithmetic, one_step(): sq_rows = jnp.sum(row_part * row_part, axis=0)  11.2 us
    another operation x3, loops' own time, tile_products(): lax.scan(one_step, start_back, jnp.arange(count, dtype=jnp.int32))  8.85 us
    dynamic_slice x12, local copies, waits for them, and re-layouts, tile_products(): lax.scan(one_step, start_back, jnp.arange(count, dtype=jnp.int32))  8 us
  transfers between devices with their start and end apart: 6, of which 0 were waited for; matrix products, arithmetic and copies ran while one was open for 81% of the time, Pallas kernels for 0%

commit v1 on v0

v1 whole, which is shorter than its diff:
```python
import jax
import jax.numpy as jnp
from jax import lax
from jax.experimental import pallas as pl
from jax.experimental.pallas import tpu as pltpu
from jax.sharding import PartitionSpec as P

F32 = jnp.float32
BF16 = jnp.bfloat16
FEATS = 64
DEPTH = 256
SIDE = 256
GROUP = 4
LOG2E = 1.4426950408889634


def three(value):
    high = value.astype(BF16).astype(F32)
    rest = value - high
    mid = rest.astype(BF16).astype(F32)
    low = (rest - mid).astype(BF16).astype(F32)
    return high, mid, low


def extra_rows(rows):
    width = rows[0].shape[1]
    which = lax.broadcasted_iota(jnp.int32, (8, width), 0)
    top = jnp.zeros((8, width), F32)
    for at, row in enumerate(rows):
        top = jnp.where(which == at, row, top)
    return jnp.concatenate([top, jnp.zeros((FEATS - 8, width), F32)], axis=0)


def half_norms(part, scale):
    scaled = part * scale
    return jnp.sum(scaled * scaled, axis=0, keepdims=True) * (-0.5 * LOG2E)


def own_side(block_ref, scale_ref, right_ref):
    scale = scale_ref[...]
    squared = scale * scale * LOG2E

    def step(at, unused):
        columns = pl.ds(pl.multiple_of(at * SIDE, SIDE), SIDE)
        part = block_ref[0:FEATS, columns]
        one = jnp.ones((1, SIDE), F32)
        weighted = three(part * squared)
        extra = extra_rows(list(three(half_norms(part, scale))) + [one, one, one])
        right_ref[:, columns] = jnp.concatenate(list(weighted) + [extra], axis=0).astype(BF16)
        return unused

    lax.fori_loop(0, block_ref.shape[1] // SIDE, step, 0)


def other_side(block_ref, scale_ref, left_ref, vec_ref):
    scale = scale_ref[...]

    def step(at, unused):
        columns = pl.ds(pl.multiple_of(at * SIDE, SIDE), SIDE)
        part = block_ref[0:FEATS, columns]
        one = jnp.ones((1, SIDE), F32)
        extra = extra_rows([one, one, one] + list(three(half_norms(part, scale))))
        whole = jnp.concatenate([part, part, part, extra], axis=0)
        left_ref[columns, :] = jnp.transpose(whole).astype(BF16)
        return unused

    lax.fori_loop(0, block_ref.shape[1] // SIDE, step, 0)
    vec_ref[...] = block_ref[FEATS:, :].astype(BF16)


def add_tile(left_ref, right_ref, vec_ref, total_ref):
    count = right_ref.shape[1]
    span = GROUP * SIDE

    def step(at, unused):
        rows_at = pl.multiple_of((at % (count // span)) * span, span)
        cols_at = pl.multiple_of((at // (count // span)) * span, span)
        for across in range(GROUP):
            columns = pl.ds(pl.multiple_of(cols_at + across * SIDE, SIDE), SIDE)
            total = total_ref[:, columns]
            for down in range(GROUP):
                rows = pl.ds(pl.multiple_of(rows_at + down * SIDE, SIDE), SIDE)
                exponent = jnp.dot(
                    left_ref[rows, :], right_ref[:, columns], preferred_element_type=F32
                )
                kern = jnp.exp2(exponent)
                high = kern.astype(BF16)
                low = (kern - high.astype(F32)).astype(BF16)
                vec = vec_ref[:, rows]
                total = total + jnp.dot(vec, high, preferred_element_type=F32)
                total = total + jnp.dot(vec, low, preferred_element_type=F32)
            total_ref[:, columns] = total
        return unused

    lax.fori_loop(0, (count // span) ** 2, step, 0)


def first_kernel(block_ref, scale_ref, right_ref, total_ref, left_ref, vec_ref):
    own_side(block_ref, scale_ref, right_ref)
    other_side(block_ref, scale_ref, left_ref, vec_ref)
    total_ref[...] = jnp.zeros_like(total_ref)
    add_tile(left_ref, right_ref, vec_ref, total_ref)


def next_kernel(block_ref, scale_ref, right_ref, before_ref, total_ref, left_ref, vec_ref):
    other_side(block_ref, scale_ref, left_ref, vec_ref)
    total_ref[...] = before_ref[...]
    add_tile(left_ref, right_ref, vec_ref, total_ref)


def scratch(count, width):
    return [pltpu.VMEM((count, DEPTH), BF16), pltpu.VMEM((width, count), BF16)]


def params():
    return pltpu.CompilerParams(vmem_limit_bytes=24 << 20)


def cost(count, width):
    return pl.CostEstimate(
        flops=2 * count * count * (DEPTH + 8 * width),
        bytes_accessed=4 << 20,
        transcendentals=count * count,
    )


def first_tile(block, scale):
    count, width = block.shape[1], block.shape[0] - FEATS
    return pl.pallas_call(
        first_kernel,
        out_shape=(
            jax.ShapeDtypeStruct((DEPTH, count), BF16),
            jax.ShapeDtypeStruct((width, count), F32),
        ),
        scratch_shapes=scratch(count, width),
        compiler_params=params(),
        cost_estimate=cost(count, width),
        name="own_tile",
    )(block, scale)


def next_tile(block, scale, right, total):
    count, width = block.shape[1], block.shape[0] - FEATS
    return pl.pallas_call(
        next_kernel,
        out_shape=jax.ShapeDtypeStruct((width, count), F32),
        scratch_shapes=scratch(count, width),
        compiler_params=params(),
        cost_estimate=cost(count, width),
        name="other_tile",
    )(block, scale, right, total)


def per_device(points, inv_scale, vectors):
    count = lax.axis_size("pts")
    block = jnp.concatenate([points.astype(F32), vectors.astype(F32)], axis=0)
    scale = inv_scale[:, None]
    pair = [(at, at ^ 1) for at in range(count)]
    near = [(at, (at - 2 if at % 2 == 0 else at + 2) % count) for at in range(count)]
    far = [(at, (at + 2 if at % 2 == 0 else at - 2) % count) for at in range(count)]
    from_near = lax.ppermute(block, "pts", near)
    from_far = lax.ppermute(block, "pts", far)
    from_pair = lax.ppermute(block, "pts", pair)
    from_both = lax.ppermute(from_near, "pts", pair)
    right, total = first_tile(block, scale)
    for other in (from_pair, from_near, from_both, from_far):
        total = next_tile(other, scale, right, total)
    return total


def solution(mesh):
    return jax.shard_map(
        per_device,
        mesh=mesh,
        in_specs=(P(None, "pts"), P(), P(None, "pts")),
        out_specs=P(None, "pts"),
        check_vma=False,
    )
```

time: 230 us -> 63.6 us (0.28)
  matrix products: 165 us -> 0 us
  Pallas kernels: 0 us -> 37.3 us
  other arithmetic: 15.7 us -> 1.08 us
  loops' own time: 8.85 us -> 0 us
  local copies, waits for them, and re-layouts: 8.13 us -> 0.1 us
  starting transfers between devices: 31 us -> 24.7 us
    dot_general x32 -> x0, matrix products: 165 us -> none  [the longest x12 71.8 us: one_step(): lax.dot_general(row_part, cols, (((0,), (0,)), ((), ())), precision=lax.P...]
    pallas_call x0 -> x5, Pallas kernels: none -> 37.3 us  [the longest x4 29.3 us: next_tile(): pl.pallas_call(next_kernel, out_shape=jax.ShapeDtypeStruct((width, count)...]
    reduce_sum x15 -> x0, other arithmetic: 13.2 us -> none  [the longest x12 11.2 us: one_step(): sq_rows = jnp.sum(row_part * row_part, axis=0)]
    another operation x3 -> x0, loops' own time: 8.85 us -> none  [tile_products(): lax.scan(one_step, start_back, jnp.arange(count, dtype=jnp.int32))]
    dynamic_slice x12 -> x0, local copies, waits for them, and re-layouts: 8 us -> none  [tile_products(): lax.scan(one_step, start_back, jnp.arange(count, dtype=jnp.int32))]
    ppermute x6 -> x4, starting transfers between devices: 31 us -> 24.7 us  [the longest x1 15.1 us: per_device(): from_pair = lax.ppermute(block, 'pts', pair)]
  transfers between devices with their start and end apart: 6 -> 4, of which waited for: 0 -> 0; matrix products, arithmetic and copies ran while one was open for 81% -> 0% of each run, Pallas kernels for 0% -> 46%
where the time goes in v1:
time: 63.6 us; the launch traced here: 63.4 us
  Pallas kernels  37.3 us (59%)
  starting transfers between devices  24.7 us (39%)
  other arithmetic  1.08 us (2%)
    pallas_call x4, Pallas kernels, next_tile(): pl.pallas_call(next_kernel, out_shape=jax.ShapeDtypeStruct((width, count)...  29.3 us
    ppermute x1, starting transfers between devices, per_device(): from_pair = lax.ppermute(block, 'pts', pair)  15.1 us
    pallas_call x1, Pallas kernels, first_tile(): pl.pallas_call(first_kernel, out_shape=(jax.ShapeDtypeStruct((DEPTH, coun...  8.03 us
    ppermute x1, starting transfers between devices, per_device(): from_near = lax.ppermute(block, 'pts', near)  4.38 us
    ppermute x1, starting transfers between devices, per_device(): from_both = lax.ppermute(from_near, 'pts', pair)  2.64 us
    ppermute x1, starting transfers between devices, per_device(): from_far = lax.ppermute(block, 'pts', far)  2.64 us
  transfers between devices with their start and end apart: 4, of which 0 were waited for; matrix products, arithmetic and copies ran while one was open for 0% of the time, Pallas kernels for 46%

profile of v1, /device:TPU:1, one launch (start us, length us, event | category | flops | bytes accessed | tf_op | source)
XLA Modules:
  0.0 63.4 jit_solution(4037685798682048602)
XLA Ops:
  0.0 1.1 %maximum_convert_fusion.block_ref = f32[96,2048]{1,0:T(8,128)S(1)} fusion(bf16[32,2048]{1,0:T(8,128)(2,1)} %param.5, bf16[64,2048]{1,0:T(8,128)(2,1)} %param.3), kind=kLoop, calls=%fused_computation | loop fusion | flops 786432 | bytes 1179648 | tf_op jit(solution)/shard_map/concatenate | solution.py:156
  1.1 0.0 copy-start
  1.1 4.4 %collective-permute-start.1 = (f32[96,2048]{1,0:T(8,128)S(1)}, f32[96,2048]{1,0:T(8,128)S(1)}, u32[]{:S(2)}, u32[]{:S(2)}) collective-permute-start(f32[96,2048]{1,0:T(8,128)S(1)} %maximum_convert_fusion.block_ref), channel_id=1, source_target_pairs={{0,510},{1,3},{2,0},{3,5},{4,2},{5,7},{6,4},{7,9},{8,6},{9,11},{10... | collective-permute-start | bytes 2359304 | tf_op jit(solution)/shard_map/ppermute | solution.py:161
  5.5 15.1 %collective-permute-start.3 = (f32[96,2048]{1,0:T(8,128)S(1)}, f32[96,2048]{1,0:T(8,128)S(1)}, u32[]{:S(2)}, u32[]{:S(2)}) collective-permute-start(f32[96,2048]{1,0:T(8,128)S(1)} %maximum_convert_fusion.block_ref), channel_id=1, source_target_pairs={{0,1},{1,0},{2,3},{3,2},{4,5},{5,4},{6,7},{7,6},{8,9},{9,8},{10,11... | collective-permute-start | bytes 2359304 | tf_op jit(solution)/shard_map/ppermute | solution.py:163
  20.6 2.6 %collective-permute-start = (f32[96,2048]{1,0:T(8,128)S(1)}, f32[96,2048]{1,0:T(8,128)S(1)}, u32[]{:S(2)}, u32[]{:S(2)}) collective-permute-start(f32[96,2048]{1,0:T(8,128)S(1)} %maximum_convert_fusion.block_ref), channel_id=1, source_target_pairs={{0,2},{1,511},{2,4},{3,1},{4,6},{5,3},{6,8},{7,5},{8,10},{9,7},{10... | collective-permute-start | bytes 2359304 | tf_op jit(solution)/shard_map/ppermute | solution.py:162
  23.2 0.0 copy-done
  23.2 0.1 copy.8.scale_ref
  23.3 8.0 %own_tile.1 = (bf16[256,2048]{1,0:T(8,128)(2,1)S(1)}, f32[32,2048]{1,0:T(8,128)S(1)}) custom-call(f32[96,2048]{1,0:T(8,128)S(1)} %maximum_convert_fusion.block_ref, f32[64,1]{1,0:T(8,128)S(1)} %copy.8.scale_ref), custom_call_target="tpu_custom_call" | custom-call | flops 4294967296 | bytes 4194304 | tf_op jit(solution)/shard_map/own_tile/pallas_call | solution.py:129
  31.4 0.0 collective-permute-done.1.block_ref
  31.4 2.6 %collective-permute-start.2 = (f32[96,2048]{1,0:T(8,128)S(1)}, f32[96,2048]{1,0:T(8,128)S(1)}, u32[]{:S(2)}, u32[]{:S(2)}) collective-permute-start(f32[96,2048]{1,0:T(8,128)S(1)} %collective-permute-done.1.block_ref), channel_id=1, source_target_pairs={{0,1},{1,0},{2,3},{3,2},{4,5},{5,4},{6,7},{7,6},{8,9},{9,8},{10,11... | collective-permute-start | bytes 2359304 | tf_op jit(solution)/shard_map/ppermute | solution.py:164
  34.0 0.0 collective-permute-done.3.block_ref
  34.0 7.1 %other_tile.4.before_ref = f32[32,2048]{1,0:T(8,128)S(1)} custom-call(f32[96,2048]{1,0:T(8,128)S(1)} %collective-permute-done.3.block_ref, f32[64,1]{1,0:T(8,128)S(1)} %copy.8.scale_ref, bf16[256,2048]{1,0:T(8,128)(2,1)S(1)} %get-tuple-element.7.right_ref, f32[32,2048]{1,0:T(8,128)S(1)} %get-tuple-element.8.before_ref), custom_call_target="tpu_custom_call" | custom-call | flops 4294967296 | bytes 4194304 | tf_op jit(solution)/shard_map/other_tile/pallas_call | solution.py:144
  41.2 7.2 %other_tile.5.before_ref = f32[32,2048]{1,0:T(8,128)S(1)} custom-call(f32[96,2048]{1,0:T(8,128)S(1)} %collective-permute-done.1.block_ref, f32[64,1]{1,0:T(8,128)S(1)} %copy.8.scale_ref, bf16[256,2048]{1,0:T(8,128)(2,1)S(1)} %get-tuple-element.7.right_ref, f32[32,2048]{1,0:T(8,128)S(1)} %other_tile.4.before_ref), custom_call_target="tpu_custom_call" | custom-call | flops 4294967296 | bytes 4194304 | tf_op jit(solution)/shard_map/other_tile/pallas_call | solution.py:144
  48.3 0.0 collective-permute-done.2.block_ref
  48.4 7.1 %other_tile.6.before_ref = f32[32,2048]{1,0:T(8,128)S(1)} custom-call(f32[96,2048]{1,0:T(8,128)S(1)} %collective-permute-done.2.block_ref, f32[64,1]{1,0:T(8,128)S(1)} %copy.8.scale_ref, bf16[256,2048]{1,0:T(8,128)(2,1)S(1)} %get-tuple-element.7.right_ref, f32[32,2048]{1,0:T(8,128)S(1)} %other_tile.5.before_ref), custom_call_target="tpu_custom_call" | custom-call | flops 4294967296 | bytes 4194304 | tf_op jit(solution)/shard_map/other_tile/pallas_call | solution.py:144
  55.5 0.0 collective-permute-done.block_ref
  55.5 7.9 %other_tile.7 = f32[32,2048]{1,0:T(8,128)} custom-call(f32[96,2048]{1,0:T(8,128)S(1)} %collective-permute-done.block_ref, f32[64,1]{1,0:T(8,128)S(1)} %copy.8.scale_ref, bf16[256,2048]{1,0:T(8,128)(2,1)S(1)} %get-tuple-element.7.right_ref, f32[32,2048]{1,0:T(8,128)S(1)} %other_tile.6.before_ref), custom_call_target="tpu_custom_call" | custom-call | flops 4294967296 | bytes 4194304 | tf_op jit(solution)/shard_map/other_tile/pallas_call | solution.py:144
Async XLA Ops:
  1.1 22.1 %copy-start = (f32[64]{0:T(128)S(1)}, f32[64]{0:T(128)}, u32[]{:S(2)}) copy-start(f32[64]{0:T(128)} %param.4) | copy-start | bytes 772
  1.1 30.3 %collective-permute-start.1 = (f32[96,2048]{1,0:T(8,128)S(1)}, f32[96,2048]{1,0:T(8,128)S(1)}, u32[]{:S(2)}, u32[]{:S(2)}) collective-permute-start(f32[96,2048]{1,0:T(8,128)S(1)} %maximum_convert_fusion.block_ref), channel_id=1, source_target_pairs={{0,510},{1,3},{2,0},{3,5},{4,2},{5,7},{6,4},{7,9},{8,6},{9,11},{10... | collective-permute-start | bytes 2359304 | tf_op jit(solution)/shard_map/ppermute | solution.py:161
  5.5 28.5 %collective-permute-start.3 = (f32[96,2048]{1,0:T(8,128)S(1)}, f32[96,2048]{1,0:T(8,128)S(1)}, u32[]{:S(2)}, u32[]{:S(2)}) collective-permute-start(f32[96,2048]{1,0:T(8,128)S(1)} %maximum_convert_fusion.block_ref), channel_id=1, source_target_pairs={{0,1},{1,0},{2,3},{3,2},{4,5},{5,4},{6,7},{7,6},{8,9},{9,8},{10,11... | collective-permute-start | bytes 2359304 | tf_op jit(solution)/shard_map/ppermute | solution.py:163
  20.6 34.9 %collective-permute-start = (f32[96,2048]{1,0:T(8,128)S(1)}, f32[96,2048]{1,0:T(8,128)S(1)}, u32[]{:S(2)}, u32[]{:S(2)}) collective-permute-start(f32[96,2048]{1,0:T(8,128)S(1)} %maximum_convert_fusion.block_ref), channel_id=1, source_target_pairs={{0,2},{1,511},{2,4},{3,1},{4,6},{5,3},{6,8},{7,5},{8,10},{9,7},{10... | collective-permute-start | bytes 2359304 | tf_op jit(solution)/shard_map/ppermute | solution.py:162
  31.4 17.0 %collective-permute-start.2 = (f32[96,2048]{1,0:T(8,128)S(1)}, f32[96,2048]{1,0:T(8,128)S(1)}, u32[]{:S(2)}, u32[]{:S(2)}) collective-permute-start(f32[96,2048]{1,0:T(8,128)S(1)} %collective-permute-done.1.block_ref), channel_id=1, source_target_pairs={{0,1},{1,0},{2,3},{3,2},{4,5},{5,4},{6,7},{7,6},{8,9},{9,8},{10,11... | collective-permute-start | bytes 2359304 | tf_op jit(solution)/shard_map/ppermute | solution.py:164

commit v2 on v1

v2 whole, which is shorter than its diff:
```python
import jax
import jax.numpy as jnp
from jax import lax
from jax.experimental import pallas as pl
from jax.experimental.pallas import tpu as pltpu
from jax.sharding import PartitionSpec as P

F32 = jnp.float32
BF16 = jnp.bfloat16
FEATS = 64
DEPTH = 256
SIDE = 256
DOWN = 4
RUN = 32
EARLY = 2
LOG2E = 1.4426950408889634


def three(value):
    high = value.astype(BF16).astype(F32)
    rest = value - high
    mid = rest.astype(BF16).astype(F32)
    low = (rest - mid).astype(BF16).astype(F32)
    return high, mid, low


def extra_rows(rows):
    width = rows[0].shape[1]
    which = lax.broadcasted_iota(jnp.int32, (8, width), 0)
    top = jnp.zeros((8, width), F32)
    for at, row in enumerate(rows):
        top = jnp.where(which == at, row, top)
    return jnp.concatenate([top, jnp.zeros((FEATS - 8, width), F32)], axis=0)


def weigh(part, squared):
    value = part * squared
    high = value.astype(BF16).astype(F32)
    mid = (value - high).astype(BF16).astype(F32)
    norm = jnp.sum(part * (high + mid), axis=0, keepdims=True) * -0.5
    return high, mid, norm


def own_side(block_ref, scale_ref, right_ref):
    squared = scale_ref[...] * scale_ref[...] * LOG2E

    def step(at, unused):
        columns = pl.ds(pl.multiple_of(at * SIDE, SIDE), SIDE)
        high, mid, norm = weigh(block_ref[0:FEATS, columns], squared)
        one = jnp.ones((1, SIDE), F32)
        extra = extra_rows(list(three(norm)) + [one, one, one])
        zero = jnp.zeros((FEATS, SIDE), F32)
        right_ref[:, columns] = jnp.concatenate([high, extra, mid, zero], axis=0).astype(BF16)
        return unused

    lax.fori_loop(0, block_ref.shape[1] // SIDE, step, 0)


def other_side(block_ref, scale_ref, left_ref, vec_ref):
    squared = scale_ref[...] * scale_ref[...] * LOG2E

    def step(at, unused):
        columns = pl.ds(pl.multiple_of(at * SIDE, SIDE), SIDE)
        part = block_ref[0:FEATS, columns]
        high, mid, norm = weigh(part, squared)
        one = jnp.ones((1, SIDE), F32)
        extra = extra_rows([one, one, one] + list(three(norm)))
        left_ref[columns, :] = jnp.transpose(jnp.concatenate([part, extra], axis=0)).astype(BF16)
        return unused

    lax.fori_loop(0, block_ref.shape[1] // SIDE, step, 0, unroll=2)
    vec_ref[...] = block_ref[FEATS:, :].astype(BF16)


def add_tile(left_ref, right_ref, vec_ref, total_ref):
    count = right_ref.shape[1]
    span = DOWN * SIDE

    def step(at, unused):
        for across in range(count // SIDE):
            columns = slice(across * SIDE, (across + 1) * SIDE)
            total = total_ref[:, columns]
            for down in range(DOWN):
                rows = pl.ds(pl.multiple_of(at * span + down * SIDE, SIDE), SIDE)
                left = left_ref[rows, :]
                exponent = jnp.dot(
                    jnp.concatenate([left, left], axis=1),
                    right_ref[:, columns],
                    preferred_element_type=F32,
                )
                kern = jnp.exp2(exponent)
                high = kern.astype(BF16)
                low = (kern - high.astype(F32)).astype(BF16)
                vec = vec_ref[:, rows]
                total = total + jnp.dot(vec, high, preferred_element_type=F32)
                total = total + jnp.dot(vec, low, preferred_element_type=F32)
            total_ref[:, columns] = total
        return unused

    lax.fori_loop(0, count // span, step, 0)


def own_tile(block_ref, scale_ref, right_ref, total_ref, left_ref, vec_ref):
    own_side(block_ref, scale_ref, right_ref)
    other_side(block_ref, scale_ref, left_ref, vec_ref)
    total_ref[...] = jnp.zeros_like(total_ref)
    add_tile(left_ref, right_ref, vec_ref, total_ref)


def before_kernel(
    flag_ref, points_ref, vectors_ref, scale_ref, block_ref, right_ref, total_ref, left_ref, vec_ref
):
    block_ref[0:FEATS, :] = points_ref[...].astype(F32)
    block_ref[FEATS:, :] = vectors_ref[...].astype(F32)

    @pl.when(flag_ref[0] == 1)
    def _():
        own_tile(block_ref, scale_ref, right_ref, total_ref, left_ref, vec_ref)


def after_kernel(
    flag_ref, block_ref, scale_ref, right_in, total_in, right_ref, total_ref, left_ref, vec_ref
):
    @pl.when(flag_ref[0] == 0)
    def _():
        own_tile(block_ref, scale_ref, right_ref, total_ref, left_ref, vec_ref)

    @pl.when(flag_ref[0] == 1)
    def _():
        right_ref[...] = right_in[...]
        total_ref[...] = total_in[...]


def next_kernel(block_ref, scale_ref, right_ref, before_ref, total_ref, left_ref, vec_ref):
    other_side(block_ref, scale_ref, left_ref, vec_ref)
    total_ref[...] = before_ref[...]
    add_tile(left_ref, right_ref, vec_ref, total_ref)


def call(body, name, outs, count, width, flops, scalars=0, inputs=0):
    specs = [pl.BlockSpec(memory_space=pltpu.SMEM)] * scalars
    specs += [pl.BlockSpec(memory_space=pltpu.VMEM)] * inputs
    return pl.pallas_call(
        body,
        in_specs=specs,
        out_shape=outs,
        scratch_shapes=[pltpu.VMEM((count, DEPTH // 2), BF16), pltpu.VMEM((width, count), BF16)],
        compiler_params=pltpu.CompilerParams(vmem_limit_bytes=24 << 20),
        cost_estimate=pl.CostEstimate(
            flops=flops, bytes_accessed=4 << 20, transcendentals=count * count
        ),
        name=name,
    )


def per_device(points, inv_scale, vectors):
    devices = lax.axis_size("pts")
    count, width = points.shape[1], vectors.shape[0]
    scale = inv_scale[:, None]
    work = 2 * count * count * (DEPTH + 8 * width)
    whole = jax.ShapeDtypeStruct((FEATS + width, count), F32)
    right_type = jax.ShapeDtypeStruct((DEPTH, count), BF16)
    total_type = jax.ShapeDtypeStruct((width, count), F32)
    flag = (lax.axis_index("pts") % RUN < EARLY).astype(jnp.int32).reshape(1)
    block, right, total = call(
        before_kernel, "own_before", (whole, right_type, total_type), count, width, 0, 1, 3
    )(flag, points, vectors, scale)
    pair = [(at, at ^ 1) for at in range(devices)]
    near = [(at, (at - 2 if at % 2 == 0 else at + 2) % devices) for at in range(devices)]
    far = [(at, (at + 2 if at % 2 == 0 else at - 2) % devices) for at in range(devices)]
    from_near = lax.ppermute(block, "pts", near)
    from_far = lax.ppermute(block, "pts", far)
    from_pair = lax.ppermute(block, "pts", pair)
    from_both = lax.ppermute(from_near, "pts", pair)
    right, total = call(
        after_kernel, "own_after", (right_type, total_type), count, width, work, 1, 4
    )(flag, block, scale, right, total)
    for other in (from_pair, from_near, from_both, from_far):
        total = call(next_kernel, "other_tile", total_type, count, width, work, 0, 4)(
            other, scale, right, total
        )
    return total


def solution(mesh):
    return jax.shard_map(
        per_device,
        mesh=mesh,
        in_specs=(P(None, "pts"), P(), P(None, "pts")),
        out_specs=P(None, "pts"),
        check_vma=False,
    )
```

time: 63.6 us -> 60.4 us (0.950)
  Pallas kernels: 37.3 us -> 31.2 us
  waiting for transfers between devices: 0.04 us -> 3.77 us
  local copies, waits for them, and re-layouts: 0.1 us -> 2.6 us
  starting transfers between devices: 24.7 us -> 22.4 us
  other arithmetic: 1.08 us -> 0 us
    pallas_call x5 -> x6, Pallas kernels: 37.3 us -> 31.2 us  [the longest x4 24.3 us: per_device(): call(next_kernel, 'other_tile', total_type, count, width, work, 0, 4)]
    ppermute x1, starting transfers between devices: 2.64 us -> 7.13 us  [per_device(): from_both = lax.ppermute(from_near, 'pts', pair)]
    ppermute x1, starting transfers between devices: 15.1 us -> 10.8 us  [per_device(): from_pair = lax.ppermute(block, 'pts', pair)]
    ppermute x1, waiting for transfers between devices: 0.01 us -> 3.74 us  [per_device(): from_near = lax.ppermute(block, 'pts', near)]
    unnamed x2 -> x6, local copies, waits for them, and re-layouts: 0.01 us -> 2.51 us
    ppermute x1, starting transfers between devices: 4.38 us -> 1.93 us  [per_device(): from_near = lax.ppermute(block, 'pts', near)]
    concatenate x1 -> x0, other arithmetic: 1.08 us -> none  [per_device(): block = jnp.concatenate([points.astype(F32), vectors.astype(F32)], axis=0)]
  transfers between devices with their start and end apart: 4 -> 4, of which waited for: 0 -> 1; matrix products, arithmetic and copies ran while one was open for 0% -> 0% of each run, Pallas kernels for 46% -> 30%
where the time goes in v2:
time: 60.4 us; the launch traced here: 60.1 us
  Pallas kernels  31.2 us (52%)
  starting transfers between devices  22.4 us (37%)
  waiting for transfers between devices  3.77 us (6%)
  local copies, waits for them, and re-layouts  2.6 us (4%)
    pallas_call x4, Pallas kernels, per_device(): call(next_kernel, 'other_tile', total_type, count, width, work, 0, 4)  24.3 us
    ppermute x1, starting transfers between devices, per_device(): from_pair = lax.ppermute(block, 'pts', pair)  10.8 us
    ppermute x1, starting transfers between devices, per_device(): from_both = lax.ppermute(from_near, 'pts', pair)  7.13 us
    pallas_call x1, Pallas kernels, per_device(): call(before_kernel, 'own_before', (whole, right_type, total_type), count,...  6.84 us
    ppermute x1, waiting for transfers between devices, per_device(): from_near = lax.ppermute(block, 'pts', near)  3.74 us
    ppermute x1, starting transfers between devices, per_device(): from_far = lax.ppermute(block, 'pts', far)  2.64 us
    unnamed x6, local copies, waits for them, and re-layouts  2.51 us
    ppermute x1, starting transfers between devices, per_device(): from_near = lax.ppermute(block, 'pts', near)  1.93 us
  transfers between devices with their start and end apart: 4, of which 1 were waited for; matrix products, arithmetic and copies ran while one was open for 0% of the time, Pallas kernels for 30%

profile of v2, /device:TPU:1, one launch (start us, length us, event | category | flops | bytes accessed | tf_op | source)
XLA Modules:
  0.0 60.1 jit_solution(11048496338334894525)
XLA Ops:
  0.0 0.0 copy-start.2
  0.0 0.7 %copy-done.2 = f32[64]{0:T(128)S(1)} copy-done((f32[64]{0:T(128)S(1)}, f32[64]{0:T(128)}, u32[]{:S(2)}) %copy-start.2) | copy-done | bytes 280
  0.7 0.1 copy.4.scale_ref
  0.8 0.0 copy-start
  0.8 0.9 %copy-done = bf16[64,2048]{1,0:T(8,128)(2,1)S(1)} copy-done((bf16[64,2048]{1,0:T(8,128)(2,1)S(1)}, bf16[64,2048]{1,0:T(8,128)(2,1)}, u32[]{:S(2)}) %copy-start) | copy-done | bytes 262168
  1.7 0.0 copy-start.1
  1.7 0.9 %copy-done.1 = bf16[32,2048]{1,0:T(8,128)(2,1)S(1)} copy-done((bf16[32,2048]{1,0:T(8,128)(2,1)S(1)}, bf16[32,2048]{1,0:T(8,128)(2,1)}, u32[]{:S(2)}) %copy-start.1) | copy-done | bytes 131096
  2.6 6.8 %own_before.1 = (f32[96,2048]{1,0:T(8,128)S(1)}, bf16[256,2048]{1,0:T(8,128)(2,1)S(1)}, f32[32,2048]{1,0:T(8,128)S(1)}) custom-call(s32[1]{0:T(128)} %bitcast.flag_ref, bf16[64,2048]{1,0:T(8,128)(2,1)S(1)} %copy-done, bf16[32,2048]{1,0:T(8,128)(2,1)S(1)} %copy-done.1, f32[64,1]{1,0:T(8,128)S(1)} %copy.4.scale_ref), custom_call_target="tpu_custom_call" | custom-call | bytes 4194304 | tf_op jit(solution)/shard_map/own_before/pallas_call | solution.py:165
  9.4 1.9 %collective-permute-start.1 = (f32[96,2048]{1,0:T(8,128)S(1)}, f32[96,2048]{1,0:T(8,128)S(1)}, u32[]{:S(2)}, u32[]{:S(2)}) collective-permute-start(f32[96,2048]{1,0:T(8,128)S(1)} %get-tuple-element.10.block_ref), channel_id=1, source_target_pairs={{0,510},{1,3},{2,0},{3,5},{4,2},{5,7},{6,4},{7,9},{8,6},{9,11},{10... | collective-permute-start | bytes 2359304 | tf_op jit(solution)/shard_map/ppermute | solution.py:171
  11.4 10.8 %collective-permute-start.3 = (f32[96,2048]{1,0:T(8,128)S(1)}, f32[96,2048]{1,0:T(8,128)S(1)}, u32[]{:S(2)}, u32[]{:S(2)}) collective-permute-start(f32[96,2048]{1,0:T(8,128)S(1)} %get-tuple-element.10.block_ref), channel_id=1, source_target_pairs={{0,1},{1,0},{2,3},{3,2},{4,5},{5,4},{6,7},{7,6},{8,9},{9,8},{10,11... | collective-permute-start | bytes 2359304 | tf_op jit(solution)/shard_map/ppermute | solution.py:173
  22.1 2.6 %collective-permute-start = (f32[96,2048]{1,0:T(8,128)S(1)}, f32[96,2048]{1,0:T(8,128)S(1)}, u32[]{:S(2)}, u32[]{:S(2)}) collective-permute-start(f32[96,2048]{1,0:T(8,128)S(1)} %get-tuple-element.10.block_ref), channel_id=1, source_target_pairs={{0,2},{1,511},{2,4},{3,1},{4,6},{5,3},{6,8},{7,5},{8,10},{9,7},{10... | collective-permute-start | bytes 2359304 | tf_op jit(solution)/shard_map/ppermute | solution.py:172
  24.8 0.1 own_after.1
  24.9 3.7 %collective-permute-done.1.block_ref = f32[96,2048]{1,0:T(8,128)S(1)} collective-permute-done((f32[96,2048]{1,0:T(8,128)S(1)}, f32[96,2048]{1,0:T(8,128)S(1)}, u32[]{:S(2)}, u32[]{:S(2)}) %collective-permute-start.1) | collective-permute-done | bytes 786464 | tf_op jit(solution)/shard_map/ppermute | solution.py:171
  28.6 7.1 %collective-permute-start.2 = (f32[96,2048]{1,0:T(8,128)S(1)}, f32[96,2048]{1,0:T(8,128)S(1)}, u32[]{:S(2)}, u32[]{:S(2)}) collective-permute-start(f32[96,2048]{1,0:T(8,128)S(1)} %collective-permute-done.1.block_ref), channel_id=1, source_target_pairs={{0,1},{1,0},{2,3},{3,2},{4,5},{5,4},{6,7},{7,6},{8,9},{9,8},{10,11... | collective-permute-start | bytes 2359304 | tf_op jit(solution)/shard_map/ppermute | solution.py:174
  35.8 0.0 collective-permute-done.3.block_ref
  35.8 5.9 %other_tile.4.before_ref = f32[32,2048]{1,0:T(8,128)S(1)} custom-call(f32[96,2048]{1,0:T(8,128)S(1)} %collective-permute-done.3.block_ref, f32[64,1]{1,0:T(8,128)S(1)} %copy.4.scale_ref, bf16[256,2048]{1,0:T(8,128)(2,1)S(1)} %get-tuple-element.13.right_ref, f32[32,2048]{1,0:T(8,128)S(1)} %get-tuple-element.14.before_ref), custom_call_target="tpu_custom_call" | custom-call | flops 4294967296 | bytes 4194304 | tf_op jit(solution)/shard_map/other_tile/pallas_call | solution.py:179
  41.7 5.9 %other_tile.5.before_ref = f32[32,2048]{1,0:T(8,128)S(1)} custom-call(f32[96,2048]{1,0:T(8,128)S(1)} %collective-permute-done.1.block_ref, f32[64,1]{1,0:T(8,128)S(1)} %copy.4.scale_ref, bf16[256,2048]{1,0:T(8,128)(2,1)S(1)} %get-tuple-element.13.right_ref, f32[32,2048]{1,0:T(8,128)S(1)} %other_tile.4.before_ref), custom_call_target="tpu_custom_call" | custom-call | flops 4294967296 | bytes 4194304 | tf_op jit(solution)/shard_map/other_tile/pallas_call | solution.py:179
  47.6 0.0 collective-permute-done.2.block_ref
  47.6 5.9 %other_tile.6.before_ref = f32[32,2048]{1,0:T(8,128)S(1)} custom-call(f32[96,2048]{1,0:T(8,128)S(1)} %collective-permute-done.2.block_ref, f32[64,1]{1,0:T(8,128)S(1)} %copy.4.scale_ref, bf16[256,2048]{1,0:T(8,128)(2,1)S(1)} %get-tuple-element.13.right_ref, f32[32,2048]{1,0:T(8,128)S(1)} %other_tile.5.before_ref), custom_call_target="tpu_custom_call" | custom-call | flops 4294967296 | bytes 4194304 | tf_op jit(solution)/shard_map/other_tile/pallas_call | solution.py:179
  53.5 0.0 collective-permute-done.block_ref
  53.5 6.6 %other_tile.7 = f32[32,2048]{1,0:T(8,128)} custom-call(f32[96,2048]{1,0:T(8,128)S(1)} %collective-permute-done.block_ref, f32[64,1]{1,0:T(8,128)S(1)} %copy.4.scale_ref, bf16[256,2048]{1,0:T(8,128)(2,1)S(1)} %get-tuple-element.13.right_ref, f32[32,2048]{1,0:T(8,128)S(1)} %other_tile.6.before_ref), custom_call_target="tpu_custom_call" | custom-call | flops 4294967296 | bytes 4194304 | tf_op jit(solution)/shard_map/other_tile/pallas_call | solution.py:179
Async XLA Ops:
  0.0 0.7 %copy-start.2 = (f32[64]{0:T(128)S(1)}, f32[64]{0:T(128)}, u32[]{:S(2)}) copy-start(f32[64]{0:T(128)} %param.4) | copy-start | bytes 772
  0.8 0.9 %copy-start = (bf16[64,2048]{1,0:T(8,128)(2,1)S(1)}, bf16[64,2048]{1,0:T(8,128)(2,1)}, u32[]{:S(2)}) copy-start(bf16[64,2048]{1,0:T(8,128)(2,1)} %points_ref.1) | copy-start | bytes 786436
  1.7 0.9 %copy-start.1 = (bf16[32,2048]{1,0:T(8,128)(2,1)S(1)}, bf16[32,2048]{1,0:T(8,128)(2,1)}, u32[]{:S(2)}) copy-start(bf16[32,2048]{1,0:T(8,128)(2,1)} %vectors_ref.1) | copy-start | bytes 393220
  9.4 19.2 %collective-permute-start.1 = (f32[96,2048]{1,0:T(8,128)S(1)}, f32[96,2048]{1,0:T(8,128)S(1)}, u32[]{:S(2)}, u32[]{:S(2)}) collective-permute-start(f32[96,2048]{1,0:T(8,128)S(1)} %get-tuple-element.10.block_ref), channel_id=1, source_target_pairs={{0,510},{1,3},{2,0},{3,5},{4,2},{5,7},{6,4},{7,9},{8,6},{9,11},{10... | collective-permute-start | bytes 2359304 | tf_op jit(solution)/shard_map/ppermute | solution.py:171
  11.4 24.4 %collective-permute-start.3 = (f32[96,2048]{1,0:T(8,128)S(1)}, f32[96,2048]{1,0:T(8,128)S(1)}, u32[]{:S(2)}, u32[]{:S(2)}) collective-permute-start(f32[96,2048]{1,0:T(8,128)S(1)} %get-tuple-element.10.block_ref), channel_id=1, source_target_pairs={{0,1},{1,0},{2,3},{3,2},{4,5},{5,4},{6,7},{7,6},{8,9},{9,8},{10,11... | collective-permute-start | bytes 2359304 | tf_op jit(solution)/shard_map/ppermute | solution.py:173
  22.1 31.4 %collective-permute-start = (f32[96,2048]{1,0:T(8,128)S(1)}, f32[96,2048]{1,0:T(8,128)S(1)}, u32[]{:S(2)}, u32[]{:S(2)}) collective-permute-start(f32[96,2048]{1,0:T(8,128)S(1)} %get-tuple-element.10.block_ref), channel_id=1, source_target_pairs={{0,2},{1,511},{2,4},{3,1},{4,6},{5,3},{6,8},{7,5},{8,10},{9,7},{10... | collective-permute-start | bytes 2359304 | tf_op jit(solution)/shard_map/ppermute | solution.py:172
  28.6 19.0 %collective-permute-start.2 = (f32[96,2048]{1,0:T(8,128)S(1)}, f32[96,2048]{1,0:T(8,128)S(1)}, u32[]{:S(2)}, u32[]{:S(2)}) collective-permute-start(f32[96,2048]{1,0:T(8,128)S(1)} %collective-permute-done.1.block_ref), channel_id=1, source_target_pairs={{0,1},{1,0},{2,3},{3,2},{4,5},{5,4},{6,7},{7,6},{8,9},{9,8},{10,11... | collective-permute-start | bytes 2359304 | tf_op jit(solution)/shard_map/ppermute | solution.py:174

commit v3 on v2

--- a/solution.py
+++ b/solution.py
@@ -108,10 +108,9 @@
 
 
 def before_kernel(
-    flag_ref, points_ref, vectors_ref, scale_ref, block_ref, right_ref, total_ref, left_ref, vec_ref
+    flag_ref, block_ref, scale_ref, again_ref, right_ref, total_ref, left_ref, vec_ref
 ):
-    block_ref[0:FEATS, :] = points_ref[...].astype(F32)
-    block_ref[FEATS:, :] = vectors_ref[...].astype(F32)
+    again_ref[...] = block_ref[...]
 
     @pl.when(flag_ref[0] == 1)
     def _():
@@ -162,23 +161,30 @@
     right_type = jax.ShapeDtypeStruct((DEPTH, count), BF16)
     total_type = jax.ShapeDtypeStruct((width, count), F32)
     flag = (lax.axis_index("pts") % RUN < EARLY).astype(jnp.int32).reshape(1)
-    block, right, total = call(
-        before_kernel, "own_before", (whole, right_type, total_type), count, width, 0, 1, 3
-    )(flag, points, vectors, scale)
     pair = [(at, at ^ 1) for at in range(devices)]
     near = [(at, (at - 2 if at % 2 == 0 else at + 2) % devices) for at in range(devices)]
     far = [(at, (at + 2 if at % 2 == 0 else at - 2) % devices) for at in range(devices)]
-    from_near = lax.ppermute(block, "pts", near)
-    from_far = lax.ppermute(block, "pts", far)
+    block = jnp.concatenate([points.astype(F32), vectors.astype(F32)], axis=0)
     from_pair = lax.ppermute(block, "pts", pair)
-    from_both = lax.ppermute(from_near, "pts", pair)
+    again, right, total = call(
+        before_kernel, "own_before", (whole, right_type, total_type), count, width, 0, 1, 2
+    )(flag, block, scale)
+    from_near = lax.ppermute(again, "pts", near)
+    from_far = lax.ppermute(again, "pts", far)
     right, total = call(
         after_kernel, "own_after", (right_type, total_type), count, width, work, 1, 4
-    )(flag, block, scale, right, total)
-    for other in (from_pair, from_near, from_both, from_far):
-        total = call(next_kernel, "other_tile", total_type, count, width, work, 0, 4)(
+    )(flag, again, scale, right, total)
+
+    def add(other, total):
+        return call(next_kernel, "other_tile", total_type, count, width, work, 0, 4)(
             other, scale, right, total
         )
+
+    total = add(from_pair, total)
+    from_near, total = lax.optimization_barrier((from_near, total))
+    from_both = lax.ppermute(from_near, "pts", pair)
+    for other in (from_near, from_both, from_far):
+        total = add(other, total)
     return total
 
 

time: 60.4 us -> 61.7 us (1.022)
  waiting for transfers between devices: 3.77 us -> 10.3 us
  starting transfers between devices: 22.4 us -> 18.1 us
  local copies, waits for them, and re-layouts: 2.6 us -> 0.75 us
  other arithmetic: 0 us -> 1.08 us
    ppermute x2, waiting for transfers between devices: 3.75 us -> 10.2 us  [the longest x1 10.2 us: per_device(): from_near = lax.ppermute(again, 'pts', near)]
    ppermute x1, starting transfers between devices: 7.13 us -> 1.91 us  [per_device(): from_both = lax.ppermute(from_near, 'pts', pair)]
    ppermute x2, starting transfers between devices: 4.56 us -> 7.4 us  [the longest x1 5.48 us: per_device(): from_far = lax.ppermute(again, 'pts', far)]
    ppermute x1, starting transfers between devices: 10.8 us -> 8.79 us  [per_device(): from_pair = lax.ppermute(block, 'pts', pair)]
    unnamed x6 -> x2, local copies, waits for them, and re-layouts: 2.51 us -> 0.65 us
    concatenate x0 -> x1, other arithmetic: none -> 1.08 us  [per_device(): block = jnp.concatenate([points.astype(F32), vectors.astype(F32)], axis=0)]
  transfers between devices with their start and end apart: 4 -> 4, of which waited for: 1 -> 1; matrix products, arithmetic and copies ran while one was open for 0% -> 0% of each run, Pallas kernels for 30% -> 40%
where the time goes in v3:
time: 61.7 us; the launch traced here: 61.5 us
  Pallas kernels  31.2 us (51%)
  starting transfers between devices  18.1 us (29%)
  waiting for transfers between devices  10.3 us (17%)
  other arithmetic  1.08 us (2%)
  local copies, waits for them, and re-layouts  0.75 us (1%)
    pallas_call x4, Pallas kernels, add(): call(next_kernel, 'other_tile', total_type, count, width, work, 0, 4)  24.3 us
    ppermute x1, waiting for transfers between devices, per_device(): from_near = lax.ppermute(again, 'pts', near)  10.2 us
    ppermute x1, starting transfers between devices, per_device(): from_pair = lax.ppermute(block, 'pts', pair)  8.79 us
    pallas_call x1, Pallas kernels, per_device(): call(before_kernel, 'own_before', (whole, right_type, total_type), count,...  6.84 us
    ppermute x1, starting transfers between devices, per_device(): from_far = lax.ppermute(again, 'pts', far)  5.48 us
    ppermute x1, starting transfers between devices, per_device(): from_near = lax.ppermute(again, 'pts', near)  1.93 us
    ppermute x1, starting transfers between devices, per_device(): from_both = lax.ppermute(from_near, 'pts', pair)  1.91 us
  transfers between devices with their start and end apart: 4, of which 1 were waited for; matrix products, arithmetic and copies ran while one was open for 0% of the time, Pallas kernels for 40%

profile of v3, /device:TPU:1, one launch (start us, length us, event | category | flops | bytes accessed | tf_op | source)
XLA Modules:
  0.0 61.5 jit_solution(5050910429368533990)
XLA Ops:
  0.0 1.1 %maximum_convert_fusion.block_ref = f32[96,2048]{1,0:T(8,128)S(1)} fusion(bf16[32,2048]{1,0:T(8,128)(2,1)} %param.5, bf16[64,2048]{1,0:T(8,128)(2,1)} %param.3), kind=kLoop, calls=%fused_computation | loop fusion | flops 786432 | bytes 1179648 | tf_op jit(solution)/shard_map/concatenate | solution.py:167
  1.1 8.8 %collective-permute-start.2 = (f32[96,2048]{1,0:T(8,128)S(1)}, f32[96,2048]{1,0:T(8,128)S(1)}, u32[]{:S(2)}, u32[]{:S(2)}) collective-permute-start(f32[96,2048]{1,0:T(8,128)S(1)} %maximum_convert_fusion.block_ref), channel_id=1, source_target_pairs={{0,1},{1,0},{2,3},{3,2},{4,5},{5,4},{6,7},{7,6},{8,9},{9,8},{10,11... | collective-permute-start | bytes 2359304 | tf_op jit(solution)/shard_map/ppermute | solution.py:168
  9.9 0.0 copy-start
  9.9 0.6 %copy-done = f32[64]{0:T(128)S(1)} copy-done((f32[64]{0:T(128)S(1)}, f32[64]{0:T(128)}, u32[]{:S(2)}) %copy-start) | copy-done | bytes 280
  10.6 0.1 copy.4.scale_ref
  10.7 6.8 %own_before.1 = (f32[96,2048]{1,0:T(8,128)S(1)}, bf16[256,2048]{1,0:T(8,128)(2,1)S(1)}, f32[32,2048]{1,0:T(8,128)S(1)}) custom-call(s32[1]{0:T(128)} %bitcast.flag_ref, f32[96,2048]{1,0:T(8,128)S(1)} %maximum_convert_fusion.block_ref, f32[64,1]{1,0:T(8,128)S(1)} %copy.4.scale_ref), custom_call_target="tpu_custom_call" | custom-call | bytes 4194304 | tf_op jit(solution)/shard_map/own_before/pallas_call | solution.py:169
  17.5 1.9 %collective-permute-start.1 = (f32[96,2048]{1,0:T(8,128)S(1)}, f32[96,2048]{1,0:T(8,128)S(1)}, u32[]{:S(2)}, u32[]{:S(2)}) collective-permute-start(f32[96,2048]{1,0:T(8,128)S(1)} %get-tuple-element.12.block_ref), channel_id=1, source_target_pairs={{0,510},{1,3},{2,0},{3,5},{4,2},{5,7},{6,4},{7,9},{8,6},{9,11},{10... | collective-permute-start | bytes 2359304 | tf_op jit(solution)/shard_map/ppermute | solution.py:172
  19.4 0.1 own_after.1
  19.5 0.0 collective-permute-done.2.block_ref
  19.5 5.9 %other_tile.4.before_ref = f32[32,2048]{1,0:T(8,128)S(1)} custom-call(f32[96,2048]{1,0:T(8,128)S(1)} %collective-permute-done.2.block_ref, f32[64,1]{1,0:T(8,128)S(1)} %copy.4.scale_ref, bf16[256,2048]{1,0:T(8,128)(2,1)S(1)} %get-tuple-element.15.right_ref, f32[32,2048]{1,0:T(8,128)S(1)} %get-tuple-element.16.before_ref), custom_call_target="tpu_custom_call" | custom-call | flops 4294967296 | bytes 4194304 | tf_op jit(solution)/shard_map/other_tile/pallas_call | solution.py:179
  25.4 10.2 %collective-permute-done.1.block_ref = f32[96,2048]{1,0:T(8,128)S(1)} collective-permute-done((f32[96,2048]{1,0:T(8,128)S(1)}, f32[96,2048]{1,0:T(8,128)S(1)}, u32[]{:S(2)}, u32[]{:S(2)}) %collective-permute-start.1) | collective-permute-done | bytes 786464 | tf_op jit(solution)/shard_map/ppermute | solution.py:172
  35.7 1.9 %collective-permute-start.3 = (f32[96,2048]{1,0:T(8,128)S(1)}, f32[96,2048]{1,0:T(8,128)S(1)}, u32[]{:S(2)}, u32[]{:S(2)}) collective-permute-start(f32[96,2048]{1,0:T(8,128)S(1)} %collective-permute-done.1.block_ref), channel_id=1, source_target_pairs={{0,1},{1,0},{2,3},{3,2},{4,5},{5,4},{6,7},{7,6},{8,9},{9,8},{10,11... | collective-permute-start | bytes 2359304 | tf_op jit(solution)/shard_map/ppermute | solution.py:185
  37.6 5.5 %collective-permute-start = (f32[96,2048]{1,0:T(8,128)S(1)}, f32[96,2048]{1,0:T(8,128)S(1)}, u32[]{:S(2)}, u32[]{:S(2)}) collective-permute-start(f32[96,2048]{1,0:T(8,128)S(1)} %get-tuple-element.12.block_ref), channel_id=1, source_target_pairs={{0,2},{1,511},{2,4},{3,1},{4,6},{5,3},{6,8},{7,5},{8,10},{9,7},{10... | collective-permute-start | bytes 2359304 | tf_op jit(solution)/shard_map/ppermute | solution.py:173
  43.1 5.9 %other_tile.5.before_ref = f32[32,2048]{1,0:T(8,128)S(1)} custom-call(f32[96,2048]{1,0:T(8,128)S(1)} %collective-permute-done.1.block_ref, f32[64,1]{1,0:T(8,128)S(1)} %copy.4.scale_ref, bf16[256,2048]{1,0:T(8,128)(2,1)S(1)} %get-tuple-element.15.right_ref, f32[32,2048]{1,0:T(8,128)S(1)} %other_tile.4.before_ref), custom_call_target="tpu_custom_call" | custom-call | flops 4294967296 | bytes 4194304 | tf_op jit(solution)/shard_map/other_tile/pallas_call | solution.py:179
  49.0 0.0 collective-permute-done.3.block_ref
  49.0 5.9 %other_tile.6.before_ref = f32[32,2048]{1,0:T(8,128)S(1)} custom-call(f32[96,2048]{1,0:T(8,128)S(1)} %collective-permute-done.3.block_ref, f32[64,1]{1,0:T(8,128)S(1)} %copy.4.scale_ref, bf16[256,2048]{1,0:T(8,128)(2,1)S(1)} %get-tuple-element.15.right_ref, f32[32,2048]{1,0:T(8,128)S(1)} %other_tile.5.before_ref), custom_call_target="tpu_custom_call" | custom-call | flops 4294967296 | bytes 4194304 | tf_op jit(solution)/shard_map/other_tile/pallas_call | solution.py:179
  54.9 0.0 collective-permute-done.block_ref
  54.9 6.6 %other_tile.7 = f32[32,2048]{1,0:T(8,128)} custom-call(f32[96,2048]{1,0:T(8,128)S(1)} %collective-permute-done.block_ref, f32[64,1]{1,0:T(8,128)S(1)} %copy.4.scale_ref, bf16[256,2048]{1,0:T(8,128)(2,1)S(1)} %get-tuple-element.15.right_ref, f32[32,2048]{1,0:T(8,128)S(1)} %other_tile.6.before_ref), custom_call_target="tpu_custom_call" | custom-call | flops 4294967296 | bytes 4194304 | tf_op jit(solution)/shard_map/other_tile/pallas_call | solution.py:179
Async XLA Ops:
  1.1 18.4 %collective-permute-start.2 = (f32[96,2048]{1,0:T(8,128)S(1)}, f32[96,2048]{1,0:T(8,128)S(1)}, u32[]{:S(2)}, u32[]{:S(2)}) collective-permute-start(f32[96,2048]{1,0:T(8,128)S(1)} %maximum_convert_fusion.block_ref), channel_id=1, source_target_pairs={{0,1},{1,0},{2,3},{3,2},{4,5},{5,4},{6,7},{7,6},{8,9},{9,8},{10,11... | collective-permute-start | bytes 2359304 | tf_op jit(solution)/shard_map/ppermute | solution.py:168
  9.9 0.7 %copy-start = (f32[64]{0:T(128)S(1)}, f32[64]{0:T(128)}, u32[]{:S(2)}) copy-start(f32[64]{0:T(128)} %param.4) | copy-start | bytes 772
  17.5 18.2 %collective-permute-start.1 = (f32[96,2048]{1,0:T(8,128)S(1)}, f32[96,2048]{1,0:T(8,128)S(1)}, u32[]{:S(2)}, u32[]{:S(2)}) collective-permute-start(f32[96,2048]{1,0:T(8,128)S(1)} %get-tuple-element.12.block_ref), channel_id=1, source_target_pairs={{0,510},{1,3},{2,0},{3,5},{4,2},{5,7},{6,4},{7,9},{8,6},{9,11},{10... | collective-permute-start | bytes 2359304 | tf_op jit(solution)/shard_map/ppermute | solution.py:172
  35.7 13.3 %collective-permute-start.3 = (f32[96,2048]{1,0:T(8,128)S(1)}, f32[96,2048]{1,0:T(8,128)S(1)}, u32[]{:S(2)}, u32[]{:S(2)}) collective-permute-start(f32[96,2048]{1,0:T(8,128)S(1)} %collective-permute-done.1.block_ref), channel_id=1, source_target_pairs={{0,1},{1,0},{2,3},{3,2},{4,5},{5,4},{6,7},{7,6},{8,9},{9,8},{10,11... | collective-permute-start | bytes 2359304 | tf_op jit(solution)/shard_map/ppermute | solution.py:185
  37.6 17.3 %collective-permute-start = (f32[96,2048]{1,0:T(8,128)S(1)}, f32[96,2048]{1,0:T(8,128)S(1)}, u32[]{:S(2)}, u32[]{:S(2)}) collective-permute-start(f32[96,2048]{1,0:T(8,128)S(1)} %get-tuple-element.12.block_ref), channel_id=1, source_target_pairs={{0,2},{1,511},{2,4},{3,1},{4,6},{5,3},{6,8},{7,5},{8,10},{9,7},{10... | collective-permute-start | bytes 2359304 | tf_op jit(solution)/shard_map/ppermute | solution.py:173

commit v4 on v3

--- a/solution.py
+++ b/solution.py
@@ -13,6 +13,7 @@
 DOWN = 4
 RUN = 32
 EARLY = 2
+WORK = 32
 LOG2E = 1.4426950408889634
 
 
@@ -146,7 +147,7 @@
         scratch_shapes=[pltpu.VMEM((count, DEPTH // 2), BF16), pltpu.VMEM((width, count), BF16)],
         compiler_params=pltpu.CompilerParams(vmem_limit_bytes=24 << 20),
         cost_estimate=pl.CostEstimate(
-            flops=flops, bytes_accessed=4 << 20, transcendentals=count * count
+            flops=flops, bytes_accessed=1 << 20, transcendentals=0
         ),
         name=name,
     )
@@ -156,19 +157,20 @@
     devices = lax.axis_size("pts")
     count, width = points.shape[1], vectors.shape[0]
     scale = inv_scale[:, None]
-    work = 2 * count * count * (DEPTH + 8 * width)
+    work = count * count * WORK
     whole = jax.ShapeDtypeStruct((FEATS + width, count), F32)
     right_type = jax.ShapeDtypeStruct((DEPTH, count), BF16)
     total_type = jax.ShapeDtypeStruct((width, count), F32)
-    flag = (lax.axis_index("pts") % RUN < EARLY).astype(jnp.int32).reshape(1)
+    index = lax.axis_index("pts")
+    flag = ((index % RUN < EARLY) & (index > 0)).astype(jnp.int32).reshape(1)
     pair = [(at, at ^ 1) for at in range(devices)]
     near = [(at, (at - 2 if at % 2 == 0 else at + 2) % devices) for at in range(devices)]
     far = [(at, (at + 2 if at % 2 == 0 else at - 2) % devices) for at in range(devices)]
     block = jnp.concatenate([points.astype(F32), vectors.astype(F32)], axis=0)
-    from_pair = lax.ppermute(block, "pts", pair)
     again, right, total = call(
         before_kernel, "own_before", (whole, right_type, total_type), count, width, 0, 1, 2
     )(flag, block, scale)
+    from_pair = lax.ppermute(again, "pts", pair)
     from_near = lax.ppermute(again, "pts", near)
     from_far = lax.ppermute(again, "pts", far)
     right, total = call(
@@ -183,8 +185,10 @@
     total = add(from_pair, total)
     from_near, total = lax.optimization_barrier((from_near, total))
     from_both = lax.ppermute(from_near, "pts", pair)
-    for other in (from_near, from_both, from_far):
-        total = add(other, total)
+    total = add(from_near, total)
+    from_far, total = lax.optimization_barrier((from_far, total))
+    total = add(from_far, total)
+    total = add(from_both, total)
     return total
 
 

time: 61.7 us -> 58.5 us (0.948)
  waiting for transfers between devices: 10.3 us -> 1.46 us
  starting transfers between devices: 18.1 us -> 23.7 us
    ppermute x1, waiting for transfers between devices: 10.2 us -> 1.43 us  [per_device(): from_near = lax.ppermute(again, 'pts', near)]
    ppermute x1, starting transfers between devices: 1.91 us -> 9.4 us  [per_device(): from_both = lax.ppermute(from_near, 'pts', pair)]
    ppermute x1, starting transfers between devices: 8.79 us -> 2.01 us  [per_device(): from_pair = lax.ppermute(again, 'pts', pair)]
    ppermute x1, starting transfers between devices: 5.48 us -> 10.4 us  [per_device(): from_far = lax.ppermute(again, 'pts', far)]
  transfers between devices with their start and end apart: 4 -> 4, of which waited for: 1 -> 1; matrix products, arithmetic and copies ran while one was open for 0% -> 0% of each run, Pallas kernels for 40% -> 30%
where the time goes in v4:
time: 58.5 us; the launch traced here: 58.3 us
  Pallas kernels  31.2 us (53%)
  starting transfers between devices  23.7 us (41%)
  waiting for transfers between devices  1.46 us (2%)
  other arithmetic  1.09 us (2%)
  local copies, waits for them, and re-layouts  0.75 us (1%)
    pallas_call x4, Pallas kernels, add(): call(next_kernel, 'other_tile', total_type, count, width, work, 0, 4)  24.3 us
    ppermute x1, starting transfers between devices, per_device(): from_far = lax.ppermute(again, 'pts', far)  10.4 us
    ppermute x1, starting transfers between devices, per_device(): from_both = lax.ppermute(from_near, 'pts', pair)  9.4 us
    pallas_call x1, Pallas kernels, per_device(): call(before_kernel, 'own_before', (whole, right_type, total_type), count,...  6.84 us
    ppermute x1, starting transfers between devices, per_device(): from_pair = lax.ppermute(again, 'pts', pair)  2.01 us
    ppermute x1, starting transfers between devices, per_device(): from_near = lax.ppermute(again, 'pts', near)  1.92 us
    ppermute x1, waiting for transfers between devices, per_device(): from_near = lax.ppermute(again, 'pts', near)  1.43 us
  transfers between devices with their start and end apart: 4, of which 1 were waited for; matrix products, arithmetic and copies ran while one was open for 0% of the time, Pallas kernels for 30%

profile of v4, /device:TPU:1, one launch (start us, length us, event | category | flops | bytes accessed | tf_op | source)
XLA Modules:
  0.0 58.3 jit_solution(4220928708453304449)
XLA Ops:
  0.0 0.0 copy-start
  0.0 0.7 %copy-done = f32[64]{0:T(128)S(1)} copy-done((f32[64]{0:T(128)S(1)}, f32[64]{0:T(128)}, u32[]{:S(2)}) %copy-start) | copy-done | bytes 280
  0.7 0.1 copy.4.scale_ref
  0.8 1.1 %maximum_convert_fusion.block_ref = f32[96,2048]{1,0:T(8,128)S(1)} fusion(bf16[32,2048]{1,0:T(8,128)(2,1)} %param.5, bf16[64,2048]{1,0:T(8,128)(2,1)} %param.3), kind=kLoop, calls=%fused_computation | loop fusion | flops 786432 | bytes 1179648 | tf_op jit(solution)/shard_map/concatenate | solution.py:169
  1.8 6.8 %own_before.1 = (f32[96,2048]{1,0:T(8,128)S(1)}, bf16[256,2048]{1,0:T(8,128)(2,1)S(1)}, f32[32,2048]{1,0:T(8,128)S(1)}) custom-call(s32[1]{0:T(128)} %bitcast.flag_ref, f32[96,2048]{1,0:T(8,128)S(1)} %maximum_convert_fusion.block_ref, f32[64,1]{1,0:T(8,128)S(1)} %copy.4.scale_ref), custom_call_target="tpu_custom_call" | custom-call | bytes 1048576 | tf_op jit(solution)/shard_map/own_before/pallas_call | solution.py:170
  8.7 2.0 %collective-permute-start.1 = (f32[96,2048]{1,0:T(8,128)S(1)}, f32[96,2048]{1,0:T(8,128)S(1)}, u32[]{:S(2)}, u32[]{:S(2)}) collective-permute-start(f32[96,2048]{1,0:T(8,128)S(1)} %get-tuple-element.14.block_ref), channel_id=1, source_target_pairs={{0,1},{1,0},{2,3},{3,2},{4,5},{5,4},{6,7},{7,6},{8,9},{9,8},{10,11... | collective-permute-start | bytes 2359304 | tf_op jit(solution)/shard_map/ppermute | solution.py:173
  10.7 1.9 %collective-permute-start = (f32[96,2048]{1,0:T(8,128)S(1)}, f32[96,2048]{1,0:T(8,128)S(1)}, u32[]{:S(2)}, u32[]{:S(2)}) collective-permute-start(f32[96,2048]{1,0:T(8,128)S(1)} %get-tuple-element.14.block_ref), channel_id=1, source_target_pairs={{0,510},{1,3},{2,0},{3,5},{4,2},{5,7},{6,4},{7,9},{8,6},{9,11},{10... | collective-permute-start | bytes 2359304 | tf_op jit(solution)/shard_map/ppermute | solution.py:174
  12.6 10.4 %collective-permute-start.3 = (f32[96,2048]{1,0:T(8,128)S(1)}, f32[96,2048]{1,0:T(8,128)S(1)}, u32[]{:S(2)}, u32[]{:S(2)}) collective-permute-start(f32[96,2048]{1,0:T(8,128)S(1)} %get-tuple-element.14.block_ref), channel_id=1, source_target_pairs={{0,2},{1,511},{2,4},{3,1},{4,6},{5,3},{6,8},{7,5},{8,10},{9,7},{10... | collective-permute-start | bytes 2359304 | tf_op jit(solution)/shard_map/ppermute | solution.py:175
  23.0 0.1 own_after.1
  23.1 0.0 collective-permute-done.1.block_ref
  23.2 5.9 %other_tile.4.before_ref = f32[32,2048]{1,0:T(8,128)S(1)} custom-call(f32[96,2048]{1,0:T(8,128)S(1)} %collective-permute-done.1.block_ref, f32[64,1]{1,0:T(8,128)S(1)} %copy.4.scale_ref, bf16[256,2048]{1,0:T(8,128)(2,1)S(1)} %get-tuple-element.17.right_ref, f32[32,2048]{1,0:T(8,128)S(1)} %get-tuple-element.18.before_ref), custom_call_target="tpu_custom_call" | custom-call | flops 134217728 | bytes 1048576 | tf_op jit(solution)/shard_map/other_tile/pallas_call | solution.py:181
  29.0 1.4 %collective-permute-done.block_ref = f32[96,2048]{1,0:T(8,128)S(1)} collective-permute-done((f32[96,2048]{1,0:T(8,128)S(1)}, f32[96,2048]{1,0:T(8,128)S(1)}, u32[]{:S(2)}, u32[]{:S(2)}) %collective-permute-start) | collective-permute-done | bytes 786464 | tf_op jit(solution)/shard_map/ppermute | solution.py:174
  30.5 9.4 %collective-permute-start.2 = (f32[96,2048]{1,0:T(8,128)S(1)}, f32[96,2048]{1,0:T(8,128)S(1)}, u32[]{:S(2)}, u32[]{:S(2)}) collective-permute-start(f32[96,2048]{1,0:T(8,128)S(1)} %collective-permute-done.block_ref), channel_id=1, source_target_pairs={{0,1},{1,0},{2,3},{3,2},{4,5},{5,4},{6,7},{7,6},{8,9},{9,8},{10,11... | collective-permute-start | bytes 2359304 | tf_op jit(solution)/shard_map/ppermute | solution.py:187
  39.9 5.9 %other_tile.5.before_ref = f32[32,2048]{1,0:T(8,128)S(1)} custom-call(f32[96,2048]{1,0:T(8,128)S(1)} %collective-permute-done.block_ref, f32[64,1]{1,0:T(8,128)S(1)} %copy.4.scale_ref, bf16[256,2048]{1,0:T(8,128)(2,1)S(1)} %get-tuple-element.17.right_ref, f32[32,2048]{1,0:T(8,128)S(1)} %other_tile.4.before_ref), custom_call_target="tpu_custom_call" | custom-call | flops 134217728 | bytes 1048576 | tf_op jit(solution)/shard_map/other_tile/pallas_call | solution.py:181
  45.8 0.0 collective-permute-done.3.block_ref
  45.8 5.9 %other_tile.6.before_ref = f32[32,2048]{1,0:T(8,128)S(1)} custom-call(f32[96,2048]{1,0:T(8,128)S(1)} %collective-permute-done.3.block_ref, f32[64,1]{1,0:T(8,128)S(1)} %copy.4.scale_ref, bf16[256,2048]{1,0:T(8,128)(2,1)S(1)} %get-tuple-element.17.right_ref, f32[32,2048]{1,0:T(8,128)S(1)} %other_tile.5.before_ref), custom_call_target="tpu_custom_call" | custom-call | flops 134217728 | bytes 1048576 | tf_op jit(solution)/shard_map/other_tile/pallas_call | solution.py:181
  51.7 0.0 collective-permute-done.2.block_ref
  51.7 6.6 %other_tile.7 = f32[32,2048]{1,0:T(8,128)} custom-call(f32[96,2048]{1,0:T(8,128)S(1)} %collective-permute-done.2.block_ref, f32[64,1]{1,0:T(8,128)S(1)} %copy.4.scale_ref, bf16[256,2048]{1,0:T(8,128)(2,1)S(1)} %get-tuple-element.17.right_ref, f32[32,2048]{1,0:T(8,128)S(1)} %other_tile.6.before_ref), custom_call_target="tpu_custom_call" | custom-call | flops 134217728 | bytes 1048576 | tf_op jit(solution)/shard_map/other_tile/pallas_call | solution.py:181
Async XLA Ops:
  0.0 0.7 %copy-start = (f32[64]{0:T(128)S(1)}, f32[64]{0:T(128)}, u32[]{:S(2)}) copy-start(f32[64]{0:T(128)} %param.4) | copy-start | bytes 772
  8.7 14.5 %collective-permute-start.1 = (f32[96,2048]{1,0:T(8,128)S(1)}, f32[96,2048]{1,0:T(8,128)S(1)}, u32[]{:S(2)}, u32[]{:S(2)}) collective-permute-start(f32[96,2048]{1,0:T(8,128)S(1)} %get-tuple-element.14.block_ref), channel_id=1, source_target_pairs={{0,1},{1,0},{2,3},{3,2},{4,5},{5,4},{6,7},{7,6},{8,9},{9,8},{10,11... | collective-permute-start | bytes 2359304 | tf_op jit(solution)/shard_map/ppermute | solution.py:173
  10.7 19.8 %collective-permute-start = (f32[96,2048]{1,0:T(8,128)S(1)}, f32[96,2048]{1,0:T(8,128)S(1)}, u32[]{:S(2)}, u32[]{:S(2)}) collective-permute-start(f32[96,2048]{1,0:T(8,128)S(1)} %get-tuple-element.14.block_ref), channel_id=1, source_target_pairs={{0,510},{1,3},{2,0},{3,5},{4,2},{5,7},{6,4},{7,9},{8,6},{9,11},{10... | collective-permute-start | bytes 2359304 | tf_op jit(solution)/shard_map/ppermute | solution.py:174
  12.6 33.1 %collective-permute-start.3 = (f32[96,2048]{1,0:T(8,128)S(1)}, f32[96,2048]{1,0:T(8,128)S(1)}, u32[]{:S(2)}, u32[]{:S(2)}) collective-permute-start(f32[96,2048]{1,0:T(8,128)S(1)} %get-tuple-element.14.block_ref), channel_id=1, source_target_pairs={{0,2},{1,511},{2,4},{3,1},{4,6},{5,3},{6,8},{7,5},{8,10},{9,7},{10... | collective-permute-start | bytes 2359304 | tf_op jit(solution)/shard_map/ppermute | solution.py:175
  30.5 21.2 %collective-permute-start.2 = (f32[96,2048]{1,0:T(8,128)S(1)}, f32[96,2048]{1,0:T(8,128)S(1)}, u32[]{:S(2)}, u32[]{:S(2)}) collective-permute-start(f32[96,2048]{1,0:T(8,128)S(1)} %collective-permute-done.block_ref), channel_id=1, source_target_pairs={{0,1},{1,0},{2,3},{3,2},{4,5},{5,4},{6,7},{7,6},{8,9},{9,8},{10,11... | collective-permute-start | bytes 2359304 | tf_op jit(solution)/shard_map/ppermute | solution.py:187

commit v5 on v4

--- a/solution.py
+++ b/solution.py
@@ -10,7 +10,7 @@
 FEATS = 64
 DEPTH = 256
 SIDE = 256
-DOWN = 4
+DOWN = 8
 RUN = 32
 EARLY = 2
 WORK = 32
@@ -61,7 +61,7 @@
     squared = scale_ref[...] * scale_ref[...] * LOG2E
 
     def step(at, unused):
-        columns = pl.ds(pl.multiple_of(at * SIDE, SIDE), SIDE)
+        columns = slice(at * SIDE, (at + 1) * SIDE)
         part = block_ref[0:FEATS, columns]
         high, mid, norm = weigh(part, squared)
         one = jnp.ones((1, SIDE), F32)
@@ -69,7 +69,8 @@
         left_ref[columns, :] = jnp.transpose(jnp.concatenate([part, extra], axis=0)).astype(BF16)
         return unused
 
-    lax.fori_loop(0, block_ref.shape[1] // SIDE, step, 0, unroll=2)
+    for at in range(block_ref.shape[1] // SIDE):
+        step(at, 0)
     vec_ref[...] = block_ref[FEATS:, :].astype(BF16)
 
 
@@ -82,7 +83,7 @@
             columns = slice(across * SIDE, (across + 1) * SIDE)
             total = total_ref[:, columns]
             for down in range(DOWN):
-                rows = pl.ds(pl.multiple_of(at * span + down * SIDE, SIDE), SIDE)
+                rows = slice(at * span + down * SIDE, at * span + (down + 1) * SIDE)
                 left = left_ref[rows, :]
                 exponent = jnp.dot(
                     jnp.concatenate([left, left], axis=1),
@@ -98,7 +99,8 @@
             total_ref[:, columns] = total
         return unused
 
-    lax.fori_loop(0, count // span, step, 0)
+    for at in range(count // span):
+        step(at, 0)
 
 
 def own_tile(block_ref, scale_ref, right_ref, total_ref, left_ref, vec_ref):

time: 58.5 us -> 55.4 us (0.947)
  Pallas kernels: 31.2 us -> 26.3 us
  starting transfers between devices: 23.7 us -> 24.6 us
  waiting for transfers between devices: 1.46 us -> 2.34 us
    pallas_call x4, Pallas kernels: 24.3 us -> 20.3 us  [add(): call(next_kernel, 'other_tile', total_type, count, width, work, 0, 4)]
    pallas_call x1, Pallas kernels: 6.84 us -> 5.77 us  [per_device(): call(before_kernel, 'own_before', (whole, right_type, total_type), count,...]
    ppermute x1, starting transfers between devices: 2.01 us -> 3.08 us  [per_device(): from_pair = lax.ppermute(again, 'pts', pair)]
    ppermute x1, waiting for transfers between devices: 1.43 us -> 2.31 us  [per_device(): from_near = lax.ppermute(again, 'pts', near)]
  transfers between devices with their start and end apart: 4 -> 4, of which waited for: 1 -> 1; matrix products, arithmetic and copies ran while one was open for 0% -> 0% of each run, Pallas kernels for 30% -> 27%
where the time goes in v5:
time: 55.4 us; the launch traced here: 55.2 us
  Pallas kernels  26.3 us (47%)
  starting transfers between devices  24.6 us (44%)
  waiting for transfers between devices  2.34 us (4%)
  other arithmetic  1.09 us (2%)
  local copies, waits for them, and re-layouts  0.75 us (1%)
    pallas_call x4, Pallas kernels, add(): call(next_kernel, 'other_tile', total_type, count, width, work, 0, 4)  20.3 us
    ppermute x1, starting transfers between devices, per_device(): from_far = lax.ppermute(again, 'pts', far)  10.4 us
    ppermute x1, starting transfers between devices, per_device(): from_both = lax.ppermute(from_near, 'pts', pair)  9.22 us
    pallas_call x1, Pallas kernels, per_device(): call(before_kernel, 'own_before', (whole, right_type, total_type), count,...  5.77 us
    ppermute x1, starting transfers between devices, per_device(): from_pair = lax.ppermute(again, 'pts', pair)  3.08 us
    ppermute x1, waiting for transfers between devices, per_device(): from_near = lax.ppermute(again, 'pts', near)  2.31 us
    ppermute x1, starting transfers between devices, per_device(): from_near = lax.ppermute(again, 'pts', near)  1.92 us
  transfers between devices with their start and end apart: 4, of which 1 were waited for; matrix products, arithmetic and copies ran while one was open for 0% of the time, Pallas kernels for 27%

profile of v5, /device:TPU:1, one launch (start us, length us, event | category | flops | bytes accessed | tf_op | source)
XLA Modules:
  0.0 55.2 jit_solution(7503887479397591731)
XLA Ops:
  0.0 0.0 copy-start
  0.0 0.7 %copy-done = f32[64]{0:T(128)S(1)} copy-done((f32[64]{0:T(128)S(1)}, f32[64]{0:T(128)}, u32[]{:S(2)}) %copy-start) | copy-done | bytes 280
  0.7 0.1 copy.4.scale_ref
  0.8 1.1 %maximum_convert_fusion.block_ref = f32[96,2048]{1,0:T(8,128)S(1)} fusion(bf16[32,2048]{1,0:T(8,128)(2,1)} %param.5, bf16[64,2048]{1,0:T(8,128)(2,1)} %param.3), kind=kLoop, calls=%fused_computation | loop fusion | flops 786432 | bytes 1179648 | tf_op jit(solution)/shard_map/concatenate | solution.py:171
  1.8 5.8 %own_before.1 = (f32[96,2048]{1,0:T(8,128)S(1)}, bf16[256,2048]{1,0:T(8,128)(2,1)S(1)}, f32[32,2048]{1,0:T(8,128)S(1)}) custom-call(s32[1]{0:T(128)} %bitcast.flag_ref, f32[96,2048]{1,0:T(8,128)S(1)} %maximum_convert_fusion.block_ref, f32[64,1]{1,0:T(8,128)S(1)} %copy.4.scale_ref), custom_call_target="tpu_custom_call" | custom-call | bytes 1048576 | tf_op jit(solution)/shard_map/own_before/pallas_call | solution.py:172
  7.6 3.1 %collective-permute-start.1 = (f32[96,2048]{1,0:T(8,128)S(1)}, f32[96,2048]{1,0:T(8,128)S(1)}, u32[]{:S(2)}, u32[]{:S(2)}) collective-permute-start(f32[96,2048]{1,0:T(8,128)S(1)} %get-tuple-element.14.block_ref), channel_id=1, source_target_pairs={{0,1},{1,0},{2,3},{3,2},{4,5},{5,4},{6,7},{7,6},{8,9},{9,8},{10,11... | collective-permute-start | bytes 2359304 | tf_op jit(solution)/shard_map/ppermute | solution.py:175
  10.7 1.9 %collective-permute-start = (f32[96,2048]{1,0:T(8,128)S(1)}, f32[96,2048]{1,0:T(8,128)S(1)}, u32[]{:S(2)}, u32[]{:S(2)}) collective-permute-start(f32[96,2048]{1,0:T(8,128)S(1)} %get-tuple-element.14.block_ref), channel_id=1, source_target_pairs={{0,510},{1,3},{2,0},{3,5},{4,2},{5,7},{6,4},{7,9},{8,6},{9,11},{10... | collective-permute-start | bytes 2359304 | tf_op jit(solution)/shard_map/ppermute | solution.py:176
  12.6 10.4 %collective-permute-start.3 = (f32[96,2048]{1,0:T(8,128)S(1)}, f32[96,2048]{1,0:T(8,128)S(1)}, u32[]{:S(2)}, u32[]{:S(2)}) collective-permute-start(f32[96,2048]{1,0:T(8,128)S(1)} %get-tuple-element.14.block_ref), channel_id=1, source_target_pairs={{0,2},{1,511},{2,4},{3,1},{4,6},{5,3},{6,8},{7,5},{8,10},{9,7},{10... | collective-permute-start | bytes 2359304 | tf_op jit(solution)/shard_map/ppermute | solution.py:177
  23.0 0.3 own_after.1
  23.3 0.0 collective-permute-done.1.block_ref
  23.3 4.8 %other_tile.4.before_ref = f32[32,2048]{1,0:T(8,128)S(1)} custom-call(f32[96,2048]{1,0:T(8,128)S(1)} %collective-permute-done.1.block_ref, f32[64,1]{1,0:T(8,128)S(1)} %copy.4.scale_ref, bf16[256,2048]{1,0:T(8,128)(2,1)S(1)} %get-tuple-element.17.right_ref, f32[32,2048]{1,0:T(8,128)S(1)} %get-tuple-element.18.before_ref), custom_call_target="tpu_custom_call" | custom-call | flops 134217728 | bytes 1048576 | tf_op jit(solution)/shard_map/other_tile/pallas_call | solution.py:183
  28.2 2.3 %collective-permute-done.block_ref = f32[96,2048]{1,0:T(8,128)S(1)} collective-permute-done((f32[96,2048]{1,0:T(8,128)S(1)}, f32[96,2048]{1,0:T(8,128)S(1)}, u32[]{:S(2)}, u32[]{:S(2)}) %collective-permute-start) | collective-permute-done | bytes 786464 | tf_op jit(solution)/shard_map/ppermute | solution.py:176
  30.5 9.2 %collective-permute-start.2 = (f32[96,2048]{1,0:T(8,128)S(1)}, f32[96,2048]{1,0:T(8,128)S(1)}, u32[]{:S(2)}, u32[]{:S(2)}) collective-permute-start(f32[96,2048]{1,0:T(8,128)S(1)} %collective-permute-done.block_ref), channel_id=1, source_target_pairs={{0,1},{1,0},{2,3},{3,2},{4,5},{5,4},{6,7},{7,6},{8,9},{9,8},{10,11... | collective-permute-start | bytes 2359304 | tf_op jit(solution)/shard_map/ppermute | solution.py:189
  39.7 4.8 %other_tile.5.before_ref = f32[32,2048]{1,0:T(8,128)S(1)} custom-call(f32[96,2048]{1,0:T(8,128)S(1)} %collective-permute-done.block_ref, f32[64,1]{1,0:T(8,128)S(1)} %copy.4.scale_ref, bf16[256,2048]{1,0:T(8,128)(2,1)S(1)} %get-tuple-element.17.right_ref, f32[32,2048]{1,0:T(8,128)S(1)} %other_tile.4.before_ref), custom_call_target="tpu_custom_call" | custom-call | flops 134217728 | bytes 1048576 | tf_op jit(solution)/shard_map/other_tile/pallas_call | solution.py:183
  44.5 0.0 collective-permute-done.3.block_ref
  44.5 4.8 %other_tile.6.before_ref = f32[32,2048]{1,0:T(8,128)S(1)} custom-call(f32[96,2048]{1,0:T(8,128)S(1)} %collective-permute-done.3.block_ref, f32[64,1]{1,0:T(8,128)S(1)} %copy.4.scale_ref, bf16[256,2048]{1,0:T(8,128)(2,1)S(1)} %get-tuple-element.17.right_ref, f32[32,2048]{1,0:T(8,128)S(1)} %other_tile.5.before_ref), custom_call_target="tpu_custom_call" | custom-call | flops 134217728 | bytes 1048576 | tf_op jit(solution)/shard_map/other_tile/pallas_call | solution.py:183
  49.4 0.0 collective-permute-done.2.block_ref
  49.4 5.8 %other_tile.7 = f32[32,2048]{1,0:T(8,128)} custom-call(f32[96,2048]{1,0:T(8,128)S(1)} %collective-permute-done.2.block_ref, f32[64,1]{1,0:T(8,128)S(1)} %copy.4.scale_ref, bf16[256,2048]{1,0:T(8,128)(2,1)S(1)} %get-tuple-element.17.right_ref, f32[32,2048]{1,0:T(8,128)S(1)} %other_tile.6.before_ref), custom_call_target="tpu_custom_call" | custom-call | flops 134217728 | bytes 1048576 | tf_op jit(solution)/shard_map/other_tile/pallas_call | solution.py:183
Async XLA Ops:
  0.0 0.7 %copy-start = (f32[64]{0:T(128)S(1)}, f32[64]{0:T(128)}, u32[]{:S(2)}) copy-start(f32[64]{0:T(128)} %param.4) | copy-start | bytes 772
  7.6 15.7 %collective-permute-start.1 = (f32[96,2048]{1,0:T(8,128)S(1)}, f32[96,2048]{1,0:T(8,128)S(1)}, u32[]{:S(2)}, u32[]{:S(2)}) collective-permute-start(f32[96,2048]{1,0:T(8,128)S(1)} %get-tuple-element.14.block_ref), channel_id=1, source_target_pairs={{0,1},{1,0},{2,3},{3,2},{4,5},{5,4},{6,7},{7,6},{8,9},{9,8},{10,11... | collective-permute-start | bytes 2359304 | tf_op jit(solution)/shard_map/ppermute | solution.py:175
  10.7 19.8 %collective-permute-start = (f32[96,2048]{1,0:T(8,128)S(1)}, f32[96,2048]{1,0:T(8,128)S(1)}, u32[]{:S(2)}, u32[]{:S(2)}) collective-permute-start(f32[96,2048]{1,0:T(8,128)S(1)} %get-tuple-element.14.block_ref), channel_id=1, source_target_pairs={{0,510},{1,3},{2,0},{3,5},{4,2},{5,7},{6,4},{7,9},{8,6},{9,11},{10... | collective-permute-start | bytes 2359304 | tf_op jit(solution)/shard_map/ppermute | solution.py:176
  12.6 31.9 %collective-permute-start.3 = (f32[96,2048]{1,0:T(8,128)S(1)}, f32[96,2048]{1,0:T(8,128)S(1)}, u32[]{:S(2)}, u32[]{:S(2)}) collective-permute-start(f32[96,2048]{1,0:T(8,128)S(1)} %get-tuple-element.14.block_ref), channel_id=1, source_target_pairs={{0,2},{1,511},{2,4},{3,1},{4,6},{5,3},{6,8},{7,5},{8,10},{9,7},{10... | collective-permute-start | bytes 2359304 | tf_op jit(solution)/shard_map/ppermute | solution.py:177
  30.5 18.9 %collective-permute-start.2 = (f32[96,2048]{1,0:T(8,128)S(1)}, f32[96,2048]{1,0:T(8,128)S(1)}, u32[]{:S(2)}, u32[]{:S(2)}) collective-permute-start(f32[96,2048]{1,0:T(8,128)S(1)} %collective-permute-done.block_ref), channel_id=1, source_target_pairs={{0,1},{1,0},{2,3},{3,2},{4,5},{5,4},{6,7},{7,6},{8,9},{9,8},{10,11... | collective-permute-start | bytes 2359304 | tf_op jit(solution)/shard_map/ppermute | solution.py:189

commit v6 on v5

--- a/solution.py
+++ b/solution.py
@@ -103,34 +103,28 @@
         step(at, 0)
 
 
-def own_tile(block_ref, scale_ref, right_ref, total_ref, left_ref, vec_ref):
-    own_side(block_ref, scale_ref, right_ref)
-    other_side(block_ref, scale_ref, left_ref, vec_ref)
-    total_ref[...] = jnp.zeros_like(total_ref)
-    add_tile(left_ref, right_ref, vec_ref, total_ref)
-
-
 def before_kernel(
     flag_ref, block_ref, scale_ref, again_ref, right_ref, total_ref, left_ref, vec_ref
 ):
     again_ref[...] = block_ref[...]
+    own_side(block_ref, scale_ref, right_ref)
+    total_ref[...] = jnp.zeros_like(total_ref)
 
     @pl.when(flag_ref[0] == 1)
     def _():
-        own_tile(block_ref, scale_ref, right_ref, total_ref, left_ref, vec_ref)
+        other_side(block_ref, scale_ref, left_ref, vec_ref)
+        add_tile(left_ref, right_ref, vec_ref, total_ref)
 
 
 def after_kernel(
-    flag_ref, block_ref, scale_ref, right_in, total_in, right_ref, total_ref, left_ref, vec_ref
+    flag_ref, block_ref, scale_ref, right_ref, before_ref, total_ref, left_ref, vec_ref
 ):
+    total_ref[...] = before_ref[...]
+
     @pl.when(flag_ref[0] == 0)
     def _():
-        own_tile(block_ref, scale_ref, right_ref, total_ref, left_ref, vec_ref)
-
-    @pl.when(flag_ref[0] == 1)
-    def _():
-        right_ref[...] = right_in[...]
-        total_ref[...] = total_in[...]
+        other_side(block_ref, scale_ref, left_ref, vec_ref)
+        add_tile(left_ref, right_ref, vec_ref, total_ref)
 
 
 def next_kernel(block_ref, scale_ref, right_ref, before_ref, total_ref, left_ref, vec_ref):
@@ -174,10 +168,6 @@
     )(flag, block, scale)
     from_pair = lax.ppermute(again, "pts", pair)
     from_near = lax.ppermute(again, "pts", near)
-    from_far = lax.ppermute(again, "pts", far)
-    right, total = call(
-        after_kernel, "own_after", (right_type, total_type), count, width, work, 1, 4
-    )(flag, again, scale, right, total)
 
     def add(other, total):
         return call(next_kernel, "other_tile", total_type, count, width, work, 0, 4)(
@@ -185,6 +175,11 @@
         )
 
     total = add(from_pair, total)
+    later, total = lax.optimization_barrier((again, total))
+    from_far = lax.ppermute(later, "pts", far)
+    total = call(after_kernel, "own_after", total_type, count, width, work, 1, 4)(
+        flag, again, scale, right, total
+    )
     from_near, total = lax.optimization_barrier((from_near, total))
     from_both = lax.ppermute(from_near, "pts", pair)
     total = add(from_near, total)

time: 55.4 us -> 52.3 us (0.944)
  starting transfers between devices: 24.6 us -> 21 us
    ppermute x1, starting transfers between devices: 9.22 us -> 4.66 us  [per_device(): from_both = lax.ppermute(from_near, 'pts', pair)]
    ppermute x1, starting transfers between devices: 3.08 us -> 3.97 us  [per_device(): from_pair = lax.ppermute(again, 'pts', pair)]
  transfers between devices with their start and end apart: 4 -> 4, of which waited for: 1 -> 1; matrix products, arithmetic and copies ran while one was open for 0% -> 0% of each run, Pallas kernels for 27% -> 29%
where the time goes in v6:
time: 52.3 us; the launch traced here: 51.5 us
  Pallas kernels  26.3 us (50%)
  starting transfers between devices  21 us (40%)
  waiting for transfers between devices  2.41 us (5%)
  other arithmetic  1.09 us (2%)
  local copies, waits for them, and re-layouts  0.75 us (1%)
    pallas_call x4, Pallas kernels, add(): call(next_kernel, 'other_tile', total_type, count, width, work, 0, 4)  20.3 us
    ppermute x1, starting transfers between devices, per_device(): from_far = lax.ppermute(later, 'pts', far)  10.4 us
    pallas_call x1, Pallas kernels, per_device(): call(before_kernel, 'own_before', (whole, right_type, total_type), count,...  5.79 us
    ppermute x1, starting transfers between devices, per_device(): from_both = lax.ppermute(from_near, 'pts', pair)  4.66 us
    ppermute x1, starting transfers between devices, per_device(): from_pair = lax.ppermute(again, 'pts', pair)  3.97 us
    ppermute x1, waiting for transfers between devices, per_device(): from_near = lax.ppermute(again, 'pts', near)  2.38 us
    ppermute x1, starting transfers between devices, per_device(): from_near = lax.ppermute(again, 'pts', near)  1.92 us
    concatenate x1, other arithmetic, per_device(): block = jnp.concatenate([points.astype(F32), vectors.astype(F32)], axis=0)  1.09 us
  transfers between devices with their start and end apart: 4, of which 1 were waited for; matrix products, arithmetic and copies ran while one was open for 0% of the time, Pallas kernels for 29%

profile of v6, /device:TPU:1, one launch (start us, length us, event | category | flops | bytes accessed | tf_op | source)
XLA Modules:
  0.0 51.5 jit_solution(7475472579314507532)
XLA Ops:
  0.0 0.0 copy-start
  0.0 0.7 %copy-done = f32[64]{0:T(128)S(1)} copy-done((f32[64]{0:T(128)S(1)}, f32[64]{0:T(128)}, u32[]{:S(2)}) %copy-start) | copy-done | bytes 280
  0.7 0.1 copy.4.scale_ref
  0.8 1.1 %maximum_convert_fusion.block_ref = f32[96,2048]{1,0:T(8,128)S(1)} fusion(bf16[32,2048]{1,0:T(8,128)(2,1)} %param.5, bf16[64,2048]{1,0:T(8,128)(2,1)} %param.3), kind=kLoop, calls=%fused_computation | loop fusion | flops 786432 | bytes 1179648 | tf_op jit(solution)/shard_map/concatenate | solution.py:165
  1.8 5.8 %own_before.1 = (f32[96,2048]{1,0:T(8,128)S(1)}, bf16[256,2048]{1,0:T(8,128)(2,1)S(1)}, f32[32,2048]{1,0:T(8,128)S(1)}) custom-call(s32[1]{0:T(128)} %bitcast.flag_ref, f32[96,2048]{1,0:T(8,128)S(1)} %maximum_convert_fusion.block_ref, f32[64,1]{1,0:T(8,128)S(1)} %copy.4.scale_ref), custom_call_target="tpu_custom_call" | custom-call | bytes 1048576 | tf_op jit(solution)/shard_map/own_before/pallas_call | solution.py:166
  7.6 4.0 %collective-permute-start.1 = (f32[96,2048]{1,0:T(8,128)S(1)}, f32[96,2048]{1,0:T(8,128)S(1)}, u32[]{:S(2)}, u32[]{:S(2)}) collective-permute-start(f32[96,2048]{1,0:T(8,128)S(1)} %get-tuple-element.19.block_ref), channel_id=1, source_target_pairs={{0,1},{1,0},{2,3},{3,2},{4,5},{5,4},{6,7},{7,6},{8,9},{9,8},{10,11... | collective-permute-start | bytes 2359304 | tf_op jit(solution)/shard_map/ppermute | solution.py:169
  11.6 1.9 %collective-permute-start = (f32[96,2048]{1,0:T(8,128)S(1)}, f32[96,2048]{1,0:T(8,128)S(1)}, u32[]{:S(2)}, u32[]{:S(2)}) collective-permute-start(f32[96,2048]{1,0:T(8,128)S(1)} %get-tuple-element.19.block_ref), channel_id=1, source_target_pairs={{0,510},{1,3},{2,0},{3,5},{4,2},{5,7},{6,4},{7,9},{8,6},{9,11},{10... | collective-permute-start | bytes 2359304 | tf_op jit(solution)/shard_map/ppermute | solution.py:170
  13.5 0.0 collective-permute-done.1.block_ref
  13.6 4.8 %other_tile.4.before_ref = f32[32,2048]{1,0:T(8,128)S(1)} custom-call(f32[96,2048]{1,0:T(8,128)S(1)} %collective-permute-done.1.block_ref, f32[64,1]{1,0:T(8,128)S(1)} %copy.4.scale_ref, bf16[256,2048]{1,0:T(8,128)(2,1)S(1)} %get-tuple-element.15.right_ref, f32[32,2048]{1,0:T(8,128)S(1)} %get-tuple-element.16.before_ref), custom_call_target="tpu_custom_call" | custom-call | flops 134217728 | bytes 1048576 | tf_op jit(solution)/shard_map/other_tile/pallas_call | solution.py:173
  18.4 10.4 %collective-permute-start.3 = (f32[96,2048]{1,0:T(8,128)S(1)}, f32[96,2048]{1,0:T(8,128)S(1)}, u32[]{:S(2)}, u32[]{:S(2)}) collective-permute-start(f32[96,2048]{1,0:T(8,128)S(1)} %get-tuple-element.19.block_ref), channel_id=1, source_target_pairs={{0,2},{1,511},{2,4},{3,1},{4,6},{5,3},{6,8},{7,5},{8,10},{9,7},{10... | collective-permute-start | bytes 2359304 | tf_op jit(solution)/shard_map/ppermute | solution.py:179
  28.8 0.2 own_after.1.before_ref
  29.0 2.4 %collective-permute-done.block_ref = f32[96,2048]{1,0:T(8,128)S(1)} collective-permute-done((f32[96,2048]{1,0:T(8,128)S(1)}, f32[96,2048]{1,0:T(8,128)S(1)}, u32[]{:S(2)}, u32[]{:S(2)}) %collective-permute-start) | collective-permute-done | bytes 786464 | tf_op jit(solution)/shard_map/ppermute | solution.py:170
  31.4 4.7 %collective-permute-start.2 = (f32[96,2048]{1,0:T(8,128)S(1)}, f32[96,2048]{1,0:T(8,128)S(1)}, u32[]{:S(2)}, u32[]{:S(2)}) collective-permute-start(f32[96,2048]{1,0:T(8,128)S(1)} %collective-permute-done.block_ref), channel_id=1, source_target_pairs={{0,1},{1,0},{2,3},{3,2},{4,5},{5,4},{6,7},{7,6},{8,9},{9,8},{10,11... | collective-permute-start | bytes 2359304 | tf_op jit(solution)/shard_map/ppermute | solution.py:184
  36.1 4.8 %other_tile.5.before_ref = f32[32,2048]{1,0:T(8,128)S(1)} custom-call(f32[96,2048]{1,0:T(8,128)S(1)} %collective-permute-done.block_ref, f32[64,1]{1,0:T(8,128)S(1)} %copy.4.scale_ref, bf16[256,2048]{1,0:T(8,128)(2,1)S(1)} %get-tuple-element.15.right_ref, f32[32,2048]{1,0:T(8,128)S(1)} %own_after.1.before_ref), custom_call_target="tpu_custom_call" | custom-call | flops 134217728 | bytes 1048576 | tf_op jit(solution)/shard_map/other_tile/pallas_call | solution.py:173
  40.9 0.0 collective-permute-done.3.block_ref
  40.9 4.8 %other_tile.6.before_ref = f32[32,2048]{1,0:T(8,128)S(1)} custom-call(f32[96,2048]{1,0:T(8,128)S(1)} %collective-permute-done.3.block_ref, f32[64,1]{1,0:T(8,128)S(1)} %copy.4.scale_ref, bf16[256,2048]{1,0:T(8,128)(2,1)S(1)} %get-tuple-element.15.right_ref, f32[32,2048]{1,0:T(8,128)S(1)} %other_tile.5.before_ref), custom_call_target="tpu_custom_call" | custom-call | flops 134217728 | bytes 1048576 | tf_op jit(solution)/shard_map/other_tile/pallas_call | solution.py:173
  45.7 0.0 collective-permute-done.2.block_ref
  45.8 5.8 %other_tile.7 = f32[32,2048]{1,0:T(8,128)} custom-call(f32[96,2048]{1,0:T(8,128)S(1)} %collective-permute-done.2.block_ref, f32[64,1]{1,0:T(8,128)S(1)} %copy.4.scale_ref, bf16[256,2048]{1,0:T(8,128)(2,1)S(1)} %get-tuple-element.15.right_ref, f32[32,2048]{1,0:T(8,128)S(1)} %other_tile.6.before_ref), custom_call_target="tpu_custom_call" | custom-call | flops 134217728 | bytes 1048576 | tf_op jit(solution)/shard_map/other_tile/pallas_call | solution.py:173
Async XLA Ops:
  0.0 0.7 %copy-start = (f32[64]{0:T(128)S(1)}, f32[64]{0:T(128)}, u32[]{:S(2)}) copy-start(f32[64]{0:T(128)} %param.4) | copy-start | bytes 772
  7.6 5.9 %collective-permute-start.1 = (f32[96,2048]{1,0:T(8,128)S(1)}, f32[96,2048]{1,0:T(8,128)S(1)}, u32[]{:S(2)}, u32[]{:S(2)}) collective-permute-start(f32[96,2048]{1,0:T(8,128)S(1)} %get-tuple-element.19.block_ref), channel_id=1, source_target_pairs={{0,1},{1,0},{2,3},{3,2},{4,5},{5,4},{6,7},{7,6},{8,9},{9,8},{10,11... | collective-permute-start | bytes 2359304 | tf_op jit(solution)/shard_map/ppermute | solution.py:169
  11.6 19.8 %collective-permute-start = (f32[96,2048]{1,0:T(8,128)S(1)}, f32[96,2048]{1,0:T(8,128)S(1)}, u32[]{:S(2)}, u32[]{:S(2)}) collective-permute-start(f32[96,2048]{1,0:T(8,128)S(1)} %get-tuple-element.19.block_ref), channel_id=1, source_target_pairs={{0,510},{1,3},{2,0},{3,5},{4,2},{5,7},{6,4},{7,9},{8,6},{9,11},{10... | collective-permute-start | bytes 2359304 | tf_op jit(solution)/shard_map/ppermute | solution.py:170
  18.4 22.5 %collective-permute-start.3 = (f32[96,2048]{1,0:T(8,128)S(1)}, f32[96,2048]{1,0:T(8,128)S(1)}, u32[]{:S(2)}, u32[]{:S(2)}) collective-permute-start(f32[96,2048]{1,0:T(8,128)S(1)} %get-tuple-element.19.block_ref), channel_id=1, source_target_pairs={{0,2},{1,511},{2,4},{3,1},{4,6},{5,3},{6,8},{7,5},{8,10},{9,7},{10... | collective-permute-start | bytes 2359304 | tf_op jit(solution)/shard_map/ppermute | solution.py:179
  31.4 14.4 %collective-permute-start.2 = (f32[96,2048]{1,0:T(8,128)S(1)}, f32[96,2048]{1,0:T(8,128)S(1)}, u32[]{:S(2)}, u32[]{:S(2)}) collective-permute-start(f32[96,2048]{1,0:T(8,128)S(1)} %collective-permute-done.block_ref), channel_id=1, source_target_pairs={{0,1},{1,0},{2,3},{3,2},{4,5},{5,4},{6,7},{7,6},{8,9},{9,8},{10,11... | collective-permute-start | bytes 2359304 | tf_op jit(solution)/shard_map/ppermute | solution.py:184

commit v7 on v6

--- a/solution.py
+++ b/solution.py
@@ -158,7 +158,7 @@
     right_type = jax.ShapeDtypeStruct((DEPTH, count), BF16)
     total_type = jax.ShapeDtypeStruct((width, count), F32)
     index = lax.axis_index("pts")
-    flag = ((index % RUN < EARLY) & (index > 0)).astype(jnp.int32).reshape(1)
+    flag = ((index % RUN < EARLY)).astype(jnp.int32).reshape(1)
     pair = [(at, at ^ 1) for at in range(devices)]
     near = [(at, (at - 2 if at % 2 == 0 else at + 2) % devices) for at in range(devices)]
     far = [(at, (at + 2 if at % 2 == 0 else at - 2) % devices) for at in range(devices)]

time: 52.3 us -> 52.3 us (level)
    ppermute x1, starting transfers between devices: 3.97 us -> 8.79 us  [per_device(): from_pair = lax.ppermute(again, 'pts', pair)]
    ppermute x1, starting transfers between devices: 4.66 us -> 1.91 us  [per_device(): from_both = lax.ppermute(from_near, 'pts', pair)]
    ppermute x1, starting transfers between devices: 10.4 us -> 8.8 us  [per_device(): from_far = lax.ppermute(later, 'pts', far)]
  transfers between devices with their start and end apart: 4 -> 4, of which waited for: 1 -> 1; matrix products, arithmetic and copies ran while one was open for 0% -> 0% of each run, Pallas kernels for 29% -> 28%
where the time goes in v7:
time: 52.3 us; the launch traced here: 52 us
  Pallas kernels  26.3 us (50%)
  starting transfers between devices  21.4 us (41%)
  waiting for transfers between devices  2.41 us (5%)
  other arithmetic  1.09 us (2%)
  local copies, waits for them, and re-layouts  0.75 us (1%)
    pallas_call x4, Pallas kernels, add(): call(next_kernel, 'other_tile', total_type, count, width, work, 0, 4)  20.3 us
    ppermute x1, starting transfers between devices, per_device(): from_far = lax.ppermute(later, 'pts', far)  8.8 us
    ppermute x1, starting transfers between devices, per_device(): from_pair = lax.ppermute(again, 'pts', pair)  8.79 us
    pallas_call x1, Pallas kernels, per_device(): call(before_kernel, 'own_before', (whole, right_type, total_type), count,...  5.79 us
    ppermute x1, waiting for transfers between devices, per_device(): from_near = lax.ppermute(again, 'pts', near)  2.38 us
    ppermute x1, starting transfers between devices, per_device(): from_near = lax.ppermute(again, 'pts', near)  1.92 us
    ppermute x1, starting transfers between devices, per_device(): from_both = lax.ppermute(from_near, 'pts', pair)  1.91 us
    concatenate x1, other arithmetic, per_device(): block = jnp.concatenate([points.astype(F32), vectors.astype(F32)], axis=0)  1.09 us
  transfers between devices with their start and end apart: 4, of which 1 were waited for; matrix products, arithmetic and copies ran while one was open for 0% of the time, Pallas kernels for 28%

profile of v7, /device:TPU:1, one launch (start us, length us, event | category | flops | bytes accessed | tf_op | source)
XLA Modules:
  0.0 52.0 jit_solution(2693969079702477238)
XLA Ops:
  0.0 0.0 copy-start
  0.0 0.7 %copy-done = f32[64]{0:T(128)S(1)} copy-done((f32[64]{0:T(128)S(1)}, f32[64]{0:T(128)}, u32[]{:S(2)}) %copy-start) | copy-done | bytes 280
  0.7 0.1 copy.4.scale_ref
  0.8 1.1 %maximum_convert_fusion.block_ref = f32[96,2048]{1,0:T(8,128)S(1)} fusion(bf16[32,2048]{1,0:T(8,128)(2,1)} %param.5, bf16[64,2048]{1,0:T(8,128)(2,1)} %param.3), kind=kLoop, calls=%fused_computation | loop fusion | flops 786432 | bytes 1179648 | tf_op jit(solution)/shard_map/concatenate | solution.py:165
  1.8 5.8 %own_before.1 = (f32[96,2048]{1,0:T(8,128)S(1)}, bf16[256,2048]{1,0:T(8,128)(2,1)S(1)}, f32[32,2048]{1,0:T(8,128)S(1)}) custom-call(s32[1]{0:T(128)} %bitcast.flag_ref, f32[96,2048]{1,0:T(8,128)S(1)} %maximum_convert_fusion.block_ref, f32[64,1]{1,0:T(8,128)S(1)} %copy.4.scale_ref), custom_call_target="tpu_custom_call" | custom-call | bytes 1048576 | tf_op jit(solution)/shard_map/own_before/pallas_call | solution.py:166
  7.6 8.8 %collective-permute-start.1 = (f32[96,2048]{1,0:T(8,128)S(1)}, f32[96,2048]{1,0:T(8,128)S(1)}, u32[]{:S(2)}, u32[]{:S(2)}) collective-permute-start(f32[96,2048]{1,0:T(8,128)S(1)} %get-tuple-element.19.block_ref), channel_id=1, source_target_pairs={{0,1},{1,0},{2,3},{3,2},{4,5},{5,4},{6,7},{7,6},{8,9},{9,8},{10,11... | collective-permute-start | bytes 2359304 | tf_op jit(solution)/shard_map/ppermute | solution.py:169
  16.4 1.9 %collective-permute-start = (f32[96,2048]{1,0:T(8,128)S(1)}, f32[96,2048]{1,0:T(8,128)S(1)}, u32[]{:S(2)}, u32[]{:S(2)}) collective-permute-start(f32[96,2048]{1,0:T(8,128)S(1)} %get-tuple-element.19.block_ref), channel_id=1, source_target_pairs={{0,510},{1,3},{2,0},{3,5},{4,2},{5,7},{6,4},{7,9},{8,6},{9,11},{10... | collective-permute-start | bytes 2359304 | tf_op jit(solution)/shard_map/ppermute | solution.py:170
  18.4 0.0 collective-permute-done.1.block_ref
  18.4 4.8 %other_tile.4.before_ref = f32[32,2048]{1,0:T(8,128)S(1)} custom-call(f32[96,2048]{1,0:T(8,128)S(1)} %collective-permute-done.1.block_ref, f32[64,1]{1,0:T(8,128)S(1)} %copy.4.scale_ref, bf16[256,2048]{1,0:T(8,128)(2,1)S(1)} %get-tuple-element.15.right_ref, f32[32,2048]{1,0:T(8,128)S(1)} %get-tuple-element.16.before_ref), custom_call_target="tpu_custom_call" | custom-call | flops 134217728 | bytes 1048576 | tf_op jit(solution)/shard_map/other_tile/pallas_call | solution.py:173
  23.2 8.8 %collective-permute-start.3 = (f32[96,2048]{1,0:T(8,128)S(1)}, f32[96,2048]{1,0:T(8,128)S(1)}, u32[]{:S(2)}, u32[]{:S(2)}) collective-permute-start(f32[96,2048]{1,0:T(8,128)S(1)} %get-tuple-element.19.block_ref), channel_id=1, source_target_pairs={{0,2},{1,511},{2,4},{3,1},{4,6},{5,3},{6,8},{7,5},{8,10},{9,7},{10... | collective-permute-start | bytes 2359304 | tf_op jit(solution)/shard_map/ppermute | solution.py:179
  32.0 0.2 own_after.1.before_ref
  32.2 2.4 %collective-permute-done.block_ref = f32[96,2048]{1,0:T(8,128)S(1)} collective-permute-done((f32[96,2048]{1,0:T(8,128)S(1)}, f32[96,2048]{1,0:T(8,128)S(1)}, u32[]{:S(2)}, u32[]{:S(2)}) %collective-permute-start) | collective-permute-done | bytes 786464 | tf_op jit(solution)/shard_map/ppermute | solution.py:170
  34.6 1.9 %collective-permute-start.2 = (f32[96,2048]{1,0:T(8,128)S(1)}, f32[96,2048]{1,0:T(8,128)S(1)}, u32[]{:S(2)}, u32[]{:S(2)}) collective-permute-start(f32[96,2048]{1,0:T(8,128)S(1)} %collective-permute-done.block_ref), channel_id=1, source_target_pairs={{0,1},{1,0},{2,3},{3,2},{4,5},{5,4},{6,7},{7,6},{8,9},{9,8},{10,11... | collective-permute-start | bytes 2359304 | tf_op jit(solution)/shard_map/ppermute | solution.py:184
  36.5 4.8 %other_tile.5.before_ref = f32[32,2048]{1,0:T(8,128)S(1)} custom-call(f32[96,2048]{1,0:T(8,128)S(1)} %collective-permute-done.block_ref, f32[64,1]{1,0:T(8,128)S(1)} %copy.4.scale_ref, bf16[256,2048]{1,0:T(8,128)(2,1)S(1)} %get-tuple-element.15.right_ref, f32[32,2048]{1,0:T(8,128)S(1)} %own_after.1.before_ref), custom_call_target="tpu_custom_call" | custom-call | flops 134217728 | bytes 1048576 | tf_op jit(solution)/shard_map/other_tile/pallas_call | solution.py:173
  41.4 0.0 collective-permute-done.3.block_ref
  41.4 4.8 %other_tile.6.before_ref = f32[32,2048]{1,0:T(8,128)S(1)} custom-call(f32[96,2048]{1,0:T(8,128)S(1)} %collective-permute-done.3.block_ref, f32[64,1]{1,0:T(8,128)S(1)} %copy.4.scale_ref, bf16[256,2048]{1,0:T(8,128)(2,1)S(1)} %get-tuple-element.15.right_ref, f32[32,2048]{1,0:T(8,128)S(1)} %other_tile.5.before_ref), custom_call_target="tpu_custom_call" | custom-call | flops 134217728 | bytes 1048576 | tf_op jit(solution)/shard_map/other_tile/pallas_call | solution.py:173
  46.2 0.0 collective-permute-done.2.block_ref
  46.2 5.8 %other_tile.7 = f32[32,2048]{1,0:T(8,128)} custom-call(f32[96,2048]{1,0:T(8,128)S(1)} %collective-permute-done.2.block_ref, f32[64,1]{1,0:T(8,128)S(1)} %copy.4.scale_ref, bf16[256,2048]{1,0:T(8,128)(2,1)S(1)} %get-tuple-element.15.right_ref, f32[32,2048]{1,0:T(8,128)S(1)} %other_tile.6.before_ref), custom_call_target="tpu_custom_call" | custom-call | flops 134217728 | bytes 1048576 | tf_op jit(solution)/shard_map/other_tile/pallas_call | solution.py:173
Async XLA Ops:
  0.0 0.7 %copy-start = (f32[64]{0:T(128)S(1)}, f32[64]{0:T(128)}, u32[]{:S(2)}) copy-start(f32[64]{0:T(128)} %param.4) | copy-start | bytes 772
  7.6 10.7 %collective-permute-start.1 = (f32[96,2048]{1,0:T(8,128)S(1)}, f32[96,2048]{1,0:T(8,128)S(1)}, u32[]{:S(2)}, u32[]{:S(2)}) collective-permute-start(f32[96,2048]{1,0:T(8,128)S(1)} %get-tuple-element.19.block_ref), channel_id=1, source_target_pairs={{0,1},{1,0},{2,3},{3,2},{4,5},{5,4},{6,7},{7,6},{8,9},{9,8},{10,11... | collective-permute-start | bytes 2359304 | tf_op jit(solution)/shard_map/ppermute | solution.py:169
  16.4 18.2 %collective-permute-start = (f32[96,2048]{1,0:T(8,128)S(1)}, f32[96,2048]{1,0:T(8,128)S(1)}, u32[]{:S(2)}, u32[]{:S(2)}) collective-permute-start(f32[96,2048]{1,0:T(8,128)S(1)} %get-tuple-element.19.block_ref), channel_id=1, source_target_pairs={{0,510},{1,3},{2,0},{3,5},{4,2},{5,7},{6,4},{7,9},{8,6},{9,11},{10... | collective-permute-start | bytes 2359304 | tf_op jit(solution)/shard_map/ppermute | solution.py:170
  23.2 18.2 %collective-permute-start.3 = (f32[96,2048]{1,0:T(8,128)S(1)}, f32[96,2048]{1,0:T(8,128)S(1)}, u32[]{:S(2)}, u32[]{:S(2)}) collective-permute-start(f32[96,2048]{1,0:T(8,128)S(1)} %get-tuple-element.19.block_ref), channel_id=1, source_target_pairs={{0,2},{1,511},{2,4},{3,1},{4,6},{5,3},{6,8},{7,5},{8,10},{9,7},{10... | collective-permute-start | bytes 2359304 | tf_op jit(solution)/shard_map/ppermute | solution.py:179
  34.6 11.6 %collective-permute-start.2 = (f32[96,2048]{1,0:T(8,128)S(1)}, f32[96,2048]{1,0:T(8,128)S(1)}, u32[]{:S(2)}, u32[]{:S(2)}) collective-permute-start(f32[96,2048]{1,0:T(8,128)S(1)} %collective-permute-done.block_ref), channel_id=1, source_target_pairs={{0,1},{1,0},{2,3},{3,2},{4,5},{5,4},{6,7},{7,6},{8,9},{9,8},{10,11... | collective-permute-start | bytes 2359304 | tf_op jit(solution)/shard_map/ppermute | solution.py:184
